TPU v7x, 256 devices: a whole 4x4x8 slice. The times are simulated.
256 devices in a mesh: seq: 16 (over y, x_hi, core), chan: 16 (over x_lo, z).
Axes of the slice: x: 4 (x_hi: 2, x_lo: 2; x = x_hi * 2 + x_lo), y: 4, z: 8, core: 2. Of those that a mesh axis runs over, the one named last changes fastest.
Arguments:
- tokens: bfloat16 [16384, 4096], P('seq', 'chan'), may hold values from -6 to 6
- in_weight: bfloat16 [3, 4096, 2048], P(None, None, 'chan'), may hold values from -0.09375 to 0.09375
- conv_weight: float32 [3, 3, 2048], P(None, None, 'chan'), may hold values from -3 to 3
- spectrum: float32 [2, 2048, 32, 1024], P(None, 'chan', 'seq'), may hold values from -6 to 6
- skip: float32 [2048], P('chan'), may hold values from -4 to 4
- out_weight: bfloat16 [2048, 4096], P('chan'), may hold values from -0.125 to 0.125
Outputs:
- mixed: bfloat16 [16384, 4096], P('seq', 'chan')
All inputs are finite; a program needn't handle non-finite values.
Results may differ from a plain program's by a relative error of at most 0.03.
Values may be sent and summed in bfloat16 or wider, within the bound.
A program may use at most 192 MiB of HBM per device.

v0:
```python
import math

import jax
import jax.numpy as jnp
from jax import lax
from jax.sharding import PartitionSpec as P

TAPS = 3


def from_behind(value, axis, by):
    size = lax.axis_size(axis)
    pairs = [(i, i + by) for i in range(size) if 0 <= i + by < size]
    return lax.ppermute(value, axis, pairs)


def angle_tables(rows_index, cols_index, modulus):
    phases = rows_index[:, None] * cols_index[None, :] % modulus
    angles = phases.astype(jnp.float32) * (2.0 * math.pi / modulus)
    return (jnp.cos(angles), jnp.sin(angles))


def split_pair(values):
    high_part = values.astype(jnp.bfloat16)
    low_part = (values - high_part.astype(jnp.float32)).astype(jnp.bfloat16)
    return (high_part, low_part)


def three_pass(form, left, right):
    left_high, left_low = split_pair(left)
    right_high, right_low = split_pair(right)
    total = jnp.einsum(form, left_high, right_high, preferred_element_type=jnp.float32)
    total = total + jnp.einsum(form, left_high, right_low, preferred_element_type=jnp.float32)
    return total + jnp.einsum(form, left_low, right_high, preferred_element_type=jnp.float32)


def apply_table(operand, table):
    return three_pass("crb,bk->crk", operand, table)


def spectral_core(real_in, imag_in, freq_list, resp_real, resp_imag, tok_rows, fft_len):
    position_index = jnp.arange(tok_rows, dtype=jnp.int32)
    twiddle_cos, twiddle_sin = angle_tables(freq_list, position_index, fft_len)
    dft_cos, dft_sin = angle_tables(position_index, position_index, tok_rows)
    turned_real = real_in * twiddle_cos + imag_in * twiddle_sin
    turned_imag = imag_in * twiddle_cos - real_in * twiddle_sin
    freq_real = apply_table(turned_real, dft_cos) + apply_table(turned_imag, dft_sin)
    freq_imag = apply_table(turned_imag, dft_cos) - apply_table(turned_real, dft_sin)
    prod_real = freq_real * resp_real - freq_imag * resp_imag
    prod_imag = freq_real * resp_imag + freq_imag * resp_real
    back_real = apply_table(prod_real, dft_cos) - apply_table(prod_imag, dft_sin)
    back_imag = apply_table(prod_imag, dft_cos) + apply_table(prod_real, dft_sin)
    shifted_real = back_real * twiddle_cos - back_imag * twiddle_sin
    shifted_imag = back_imag * twiddle_cos + back_real * twiddle_sin
    return (shifted_real, shifted_imag)


def shards(tokens, in_weight, conv_weight, spectrum, skip, out_weight):
    tok_rows = tokens.shape[0]
    seq_count = lax.axis_size("seq")
    seq_index = lax.axis_index("seq")
    fft_len = 2 * seq_count * tok_rows
    freq_blocks = 2 * seq_count
    norm_factor = 1.0 / fft_len
    projected = jnp.einsum(
        "td,pdc->pct",
        lax.all_gather(tokens, "chan", axis=1, tiled=True),
        in_weight,
        preferred_element_type=jnp.float32,
    ).astype(jnp.bfloat16)
    margin = TAPS - 1
    earlier = from_behind(projected[:, :, tok_rows - margin :], "seq", 1)
    extended = jnp.concatenate([earlier, projected], axis=2).astype(jnp.float32)
    filtered = conv_weight[0][:, :, None] * extended[:, :, margin : margin + tok_rows]
    for tap_index in range(1, TAPS):
        filtered = (
            filtered
            + conv_weight[tap_index][:, :, None]
            * extended[:, :, margin - tap_index : margin - tap_index + tok_rows]
        )
    query_rows = filtered[0]
    signal = (filtered[1] * filtered[2]).astype(jnp.bfloat16)
    source_index = jnp.arange(seq_count, dtype=jnp.int32)
    freq_index = jnp.arange(freq_blocks, dtype=jnp.int32)
    cross_cos, cross_sin = angle_tables(source_index, freq_index, freq_blocks)
    values = lax.all_to_all(
        signal[:, None, :], "seq", split_axis=2, concat_axis=1, tiled=True
    ).astype(jnp.float32)
    real_part = three_pass("iab,ak->ikb", values, cross_cos)
    imag_part = -three_pass("iab,ak->ikb", values, cross_sin)
    stacked = jnp.stack([real_part, imag_part], axis=1)
    spectral = lax.all_to_all(
        stacked.astype(jnp.bfloat16), "seq", split_axis=2, concat_axis=3, tiled=True
    ).astype(stacked.dtype)
    own_freq = 2 * seq_index + jnp.arange(2, dtype=jnp.int32)
    shifted_real, shifted_imag = spectral_core(
        spectral[:, 0], spectral[:, 1], own_freq, spectrum[0], spectrum[1], tok_rows, fft_len
    )
    rows_index = jnp.arange(lax.axis_size("seq") * 1, dtype=jnp.int32)
    part_cos, part_sin = angle_tables(rows_index, own_freq, freq_blocks)
    partial_terms = three_pass("ar,crb->acb", part_cos, shifted_real)
    partial_terms = partial_terms - three_pass("ar,crb->acb", part_sin, shifted_imag)
    longconv = lax.psum_scatter(
        (partial_terms * norm_factor).astype(jnp.bfloat16), "seq", scatter_dimension=0, tiled=True
    ).astype(jnp.float32)[0]
    gated = (query_rows * (longconv + skip[:, None] * signal.astype(jnp.float32))).astype(
        jnp.bfloat16
    )
    partial_terms = lax.dot_general(
        gated, out_weight, (((0,), (0,)), ((), ())), preferred_element_type=jnp.float32
    )
    result = lax.psum_scatter(
        partial_terms.astype(jnp.bfloat16), "chan", scatter_dimension=1, tiled=True
    )
    return result


def solution(mesh):
    placed = (
        P("seq", "chan"),
        P(None, None, "chan"),
        P(None, None, "chan"),
        P(None, "chan", "seq", None),
        P("chan"),
        P("chan", None),
    )
    return jax.shard_map(
        shards, mesh=mesh, in_specs=placed, out_specs=P("seq", "chan"), check_vma=False
    )
```

profile of v0, /device:TPU:2, one launch (start us, length us, event | category | flops | bytes accessed | tf_op | source)
XLA Modules:
  0.0 867.0 jit_solution(11361406905913467194)
XLA Ops:
  7.3 129.1 %all-gather.2.cloned.1.call-done = bf16[1024,4096]{1,0:T(8,128)(2,1)} async-done(((bf16[1024,256]{1,0:T(8,128)(2,1)}), bf16[1024,4096]{1,0:T(8,128)(2,1)}) %all-gather.2.cloned.1.call-update) | async-done | bytes 8388624 | tf_op jit(solution)/shard_map/all_gather | solution.py:67
  150.6 20.0 %all_to_all.21 = bf16[16,2,4096]{2,1,0:T(2,128)(2,1)S(1)} all-to-all(bf16[16,2,4096]{2,1,0:T(2,128)(2,1)S(1)} %reshape.113), channel_id=1, replica_groups=mesh['seq'=16,'chan'=16] {'seq'}, dimensions={0} | all-to-all | bytes 524288 | tf_op jit(solution)/shard_map/all_to_all | solution.py:86
  200.4 16.3 %fusion.21 = f32[128,2,1024]{2,0,1:T(8,128)S(1)} fusion(bf16[128,2,1024]{2,0,1:T(8,128)(2,1)S(1)} %get-tuple-element.5), kind=kOutput, calls=%fused_computation.32 | convolution fusion | flops 552599552 | bytes 1572864 | tf_op jit(solution)/shard_map/crb,bk->crk/dot_general | solution.py:34
  216.7 16.1 %fusion.41 = f32[128,2,1024]{2,0,1:T(8,128)S(1)} fusion(bf16[128,2,1024]{2,0,1:T(8,128)(2,1)S(1)} %get-tuple-element.5), kind=kOutput, calls=%fused_computation.52 | convolution fusion | flops 552599552 | bytes 1572864 | tf_op jit(solution)/shard_map/crb,bk->crk/dot_general | solution.py:34
  232.8 16.5 %fusion.37 = f32[128,2,1024]{2,0,1:T(8,128)S(1)} fusion(bf16[128,2,1024]{2,0,1:T(8,128)(2,1)S(1)} %get-tuple-element.15), kind=kOutput, calls=%fused_computation.48 | convolution fusion | flops 552599552 | bytes 1572864 | tf_op jit(solution)/shard_map/crb,bk->crk/dot_general | solution.py:34
  249.3 16.3 %fusion.25 = f32[128,2,1024]{2,0,1:T(8,128)S(1)} fusion(bf16[128,2,1024]{2,0,1:T(8,128)(2,1)S(1)} %get-tuple-element.15), kind=kOutput, calls=%fused_computation.36 | convolution fusion | flops 552599552 | bytes 1572864 | tf_op jit(solution)/shard_map/crb,bk->crk/dot_general | solution.py:34
  265.6 16.4 %fusion.23 = f32[128,2,1024]{2,0,1:T(8,128)S(1)} fusion(bf16[128,2,1024]{2,0,1:T(8,128)(2,1)S(1)} %get-tuple-element.6), kind=kOutput, calls=%fused_computation.34 | convolution fusion | flops 552599552 | bytes 1572864 | tf_op jit(solution)/shard_map/crb,bk->crk/dot_general | solution.py:32
  282.0 16.1 %fusion.43 = f32[128,2,1024]{2,0,1:T(8,128)S(1)} fusion(bf16[128,2,1024]{2,0,1:T(8,128)(2,1)S(1)} %get-tuple-element.6), kind=kOutput, calls=%fused_computation.54 | convolution fusion | flops 552599552 | bytes 1572864 | tf_op jit(solution)/shard_map/crb,bk->crk/dot_general | solution.py:32
  298.2 16.5 %fusion.27 = f32[128,2,1024]{2,0,1:T(8,128)S(1)} fusion(bf16[128,2,1024]{2,0,1:T(8,128)(2,1)S(1)} %get-tuple-element.16), kind=kOutput, calls=%fused_computation.38 | convolution fusion | flops 552599552 | bytes 1572864 | tf_op jit(solution)/shard_map/crb,bk->crk/dot_general | solution.py:32
  314.6 16.1 %fusion.39 = f32[128,2,1024]{2,0,1:T(8,128)S(1)} fusion(bf16[128,2,1024]{2,0,1:T(8,128)(2,1)S(1)} %get-tuple-element.16), kind=kOutput, calls=%fused_computation.50 | convolution fusion | flops 552599552 | bytes 1572864 | tf_op jit(solution)/shard_map/crb,bk->crk/dot_general | solution.py:32
  330.8 16.7 %fusion.90 = f32[128,2,1024]{2,0,1:T(8,128)S(1)} fusion(f32[128,2,1024]{2,0,1:T(8,128)S(1)} %fusion.41, f32[128,2,1024]{2,0,1:T(8,128)S(1)} %fusion.43, bf16[128,2,1024]{2,0,1:T(8,128)(2,1)S(1)} %get-tuple-element.6), kind=kOutput, calls=%fused_computation.80 | convolution fusion | flops 556269568 | bytes 3670016 | tf_op jit(solution)/shard_map/crb,bk->crk/dot_general | solution.py:33
  347.5 16.5 %fusion.96 = f32[128,2,1024]{2,0,1:T(8,128)S(1)} fusion(f32[128,2,1024]{2,0,1:T(8,128)S(1)} %fusion.37, f32[128,2,1024]{2,0,1:T(8,128)S(1)} %fusion.39, bf16[128,2,1024]{2,0,1:T(8,128)(2,1)S(1)} %get-tuple-element.16), kind=kOutput, calls=%fused_computation.82 | convolution fusion | flops 556269568 | bytes 3670016 | tf_op jit(solution)/shard_map/crb,bk->crk/dot_general | solution.py:33
  364.0 17.1 %fusion.144 = f32[128,2,1024]{2,0,1:T(8,128)S(1)} fusion(f32[128,2,1024]{2,0,1:T(8,128)S(1)} %fusion.90, f32[128,2,1024]{2,0,1:T(8,128)S(1)} %fusion.25, f32[128,2,1024]{2,0,1:T(8,128)S(1)} %fusion.27, bf16[128,2,1024]{2,0,1:T(8,128)(2,1)S(1)} %get-tuple-element.16), kind=kOutput, calls=%fused_computation.98 | convolution fusion | flops 556531712 | bytes 4718592 | tf_op jit(solution)/shard_map/crb,bk->crk/dot_general | solution.py:33
  381.2 17.5 %multiply_add_fusion.1 = (f32[128,2,1024]{2,0,1:T(8,128)S(1)}, f32[128,2,1024]{2,0,1:T(8,128)S(1)}) fusion(f32[128,2,1024]{2,0,1:T(8,128)S(1)} %fusion.144, f32[1,128,2,1024]{3,2,1,0:T(2,128)S(1)} %copy-done.6, f32[1,128,2,1024]{3,2,1,0:T(2,128)S(1)} %copy-done.5, f32[128,2,1024]{2,0,1:T(8,128)S(1)} %fusion.96, f32[128,2,1024]{2,0,1:T(8,128)S(1)} %fusion.21, ...), kind=kOutput, calls=%fused_computation.117 | convolution fusion | flops 558104576 | bytes 8912896 | tf_op jit(solution)/shard_map/crb,bk->crk/dot_general | solution.py:33
  414.5 16.0 %fusion.29 = f32[128,2,1024]{2,0,1:T(8,128)S(1)} fusion(f32[128,2,1024]{2,0,1:T(8,128)S(1)} %get-tuple-element.9), kind=kOutput, calls=%fused_computation.40 | convolution fusion | flops 553648128 | bytes 2097152 | tf_op jit(solution)/shard_map/crb,bk->crk/dot_general | solution.py:34
  430.5 16.1 %fusion.17 = f32[128,2,1024]{2,0,1:T(8,128)S(1)} fusion(f32[128,2,1024]{2,0,1:T(8,128)S(1)} %get-tuple-element.9), kind=kOutput, calls=%fused_computation.28 | convolution fusion | flops 553648128 | bytes 2097152 | tf_op jit(solution)/shard_map/crb,bk->crk/dot_general | solution.py:34
  446.6 16.1 %fusion.19 = f32[128,2,1024]{2,0,1:T(8,128)S(1)} fusion(f32[128,2,1024]{2,0,1:T(8,128)S(1)} %get-tuple-element.9), kind=kOutput, calls=%fused_computation.30 | convolution fusion | flops 552861696 | bytes 2097152 | tf_op jit(solution)/shard_map/crb,bk->crk/dot_general | solution.py:32
  478.6 16.4 %fusion.13 = f32[128,2,1024]{2,0,1:T(8,128)S(1)} fusion(f32[128,2,1024]{2,0,1:T(8,128)S(1)} %get-tuple-element.10), kind=kOutput, calls=%fused_computation.24 | convolution fusion | flops 553648128 | bytes 2097152 | tf_op jit(solution)/shard_map/crb,bk->crk/dot_general | solution.py:34
  526.6 16.3 %fusion.108 = f32[128,2,1024]{2,0,1:T(8,128)S(1)} fusion(f32[128,2,1024]{2,0,1:T(8,128)S(1)} %fusion.29, f32[128,2,1024]{2,0,1:T(8,128)S(1)} %fusion.31, f32[128,2,1024]{2,0,1:T(8,128)S(1)} %get-tuple-element.9), kind=kOutput, calls=%fused_computation.86 | convolution fusion | flops 556531712 | bytes 4194304 | tf_op jit(solution)/shard_map/crb,bk->crk/dot_general | solution.py:33
  558.9 16.3 %fusion.138 = f32[128,2,1024]{2,0,1:T(8,128)S(1)} fusion(f32[128,2,1024]{2,0,1:T(8,128)S(1)} %fusion.102, f32[128,2,1024]{2,0,1:T(8,128)S(1)} %fusion.17, f32[128,2,1024]{2,0,1:T(8,128)S(1)} %fusion.19, f32[128,2,1024]{2,0,1:T(8,128)S(1)} %get-tuple-element.9), kind=kOutput, calls=%fused_computation.96 | convolution fusion | flops 556793856 | bytes 5242880 | tf_op jit(solution)/shard_map/crb,bk->crk/dot_general | solution.py:33
  575.3 16.9 %subtract_convert_fusion.3 = (bf16[128,2,1024]{2,0,1:T(8,128)(2,1)S(1)}, bf16[128,2,1024]{2,0,1:T(8,128)(2,1)S(1)}, bf16[128,2,1024]{2,0,1:T(8,128)(2,1)S(1)}, bf16[128,2,1024]{2,0,1:T(8,128)(2,1)S(1)}) fusion(f32[2,1024]{1,0:T(2,128)S(1)} %get-tuple-element.25, f32[128,2,1024]{2,0,1:T(8,128)S(1)} %fusion.138, f32[2,1024]{1,0:T(2,128)S(1)} %get-tuple-element.24, ...), kind=kOutput, calls=%fused_computation.114 | convolution fusion | flops 560463872 | bytes 7356416 | tf_op jit(solution)/shard_map/crb,bk->crk/dot_general | solution.py:33
  617.4 52.4 %fusion.4 = bf16[16,128,1024]{2,1,0:T(8,128)(2,1)} fusion(f32[16,128,1024]{2,0,1:T(8,128)} %fusion.165, f32[16,128,1024]{2,0,1:T(8,128)} %fusion.157, f32[16,128,1024]{2,0,1:T(8,128)} %fusion.167, f32[16,128,1024]{2,0,1:T(8,128)} %fusion.169, f32[16,128,1024]{2,0,1:T(8,128)} %fusion.159, f32[16,128,1024]{2,0,1:T(8,128)} %fusion.171), kind=kLoop, calls=%fused_computation.5 | loop fusion | flops 14680064 | bytes 54525952 | tf_op jit(solution)/shard_map/convert_element_type | solution.py:104
  669.9 83.3 %reduce-scatter.3.cloned.1.call-done = bf16[1,128,1024]{2,1,0:T(8,128)(2,1)} async-done(((bf16[16,128,1024]{2,1,0:T(8,128)(2,1)}), bf16[1,128,1024]{2,1,0:T(8,128)(2,1)}) %reduce-scatter.3.cloned.1.call-update) | async-done | bytes 262160 | tf_op jit(solution)/shard_map/reduce_scatter | solution.py:103
  759.9 100.2 %reduce-scatter.5.cloned.1.call-done = bf16[1024,256]{1,0:T(8,128)(2,1)} async-done(((bf16[1024,4096]{1,0:T(8,128)(2,1)}), bf16[1024,256]{1,0:T(8,128)(2,1)}) %reduce-scatter.5.cloned.1.call-update) | async-done | bytes 524304 | tf_op jit(solution)/shard_map/reduce_scatter | solution.py:112
  (71 shorter events, 155.9 us)
Async XLA Ops:
  6.5 129.8 %copy-start = (bf16[3,4096,128]{2,1,0:T(8,128)(2,1)S(1)}, bf16[3,4096,128]{2,1,0:T(8,128)(2,1)}, u32[]{:S(2)}) copy-start(bf16[3,4096,128]{2,1,0:T(8,128)(2,1)} %param.7) | copy-start | bytes 9437188
  6.5 129.8 %all-gather.2.cloned.1.call-start = ((), (), s32[]{:S(2)}) async-start(), calls=%async_computation.4 | async-start | bytes 8912896 | tf_op jit(solution)/shard_map/all_gather | solution.py:67
  7.3 136.5 %copy-start.7 = (f32[3,3,128]{2,1,0:T(4,128)S(1)}, f32[3,3,128]{2,1,0:T(4,128)}, u32[]{:S(2)}) copy-start(f32[3,3,128]{2,1,0:T(4,128)} %param.8) | copy-start | bytes 13828
  142.5 2.2 collective-permute-start
  146.2 1.1 copy-start.2
  174.8 21.7 %all-to-all-start.1 = ((bf16[128,2,32,64]{0,3,1,2:T(8,128)(2,1)}), bf16[128,2,32,64]{0,3,1,2:T(8,128)(2,1)S(1)}, u32[]{:S(2)}, u32[]{:S(2)}) async-start(bf16[128,2,32,64]{0,3,1,2:T(8,128)(2,1)} %copy.86), calls=%async_computation.1 | async-start | bytes 2097152 | tf_op jit(solution)/shard_map/all_to_all | solution.py:92
  178.5 574.7 %reduce-scatter.3.cloned.1.call-start = ((), (), s32[]{:S(2)}) async-start(), calls=%async_computation.5 | async-start | bytes 4456448 | tf_op jit(solution)/shard_map/reduce_scatter | solution.py:103
  364.0 17.2 %copy-start.5 = (f32[1,128,2,1024]{3,2,1,0:T(2,128)S(1)}, f32[1,128,2,1024]{3,2,1,0:T(2,128)}, u32[]{:S(2)}) copy-start(f32[1,128,2,1024]{3,2,1,0:T(2,128)} %get-tuple-element.17) | copy-start | bytes 3145732
  364.0 17.2 %copy-start.6 = (f32[1,128,2,1024]{3,2,1,0:T(2,128)S(1)}, f32[1,128,2,1024]{3,2,1,0:T(2,128)}, u32[]{:S(2)}) copy-start(f32[1,128,2,1024]{3,2,1,0:T(2,128)} %get-tuple-element.18) | copy-start | bytes 3145732
  669.8 83.4 %copy-start.3 = (f32[3,128,1024]{2,1,0:T(8,128)S(1)}, f32[3,128,1024]{2,1,0:T(8,128)}, u32[]{:S(2)}) copy-start(f32[3,128,1024]{2,1,0:T(8,128)} %copy-done.2) | copy-start | bytes 4718596
  669.8 83.4 %copy-start.4 = (bf16[128,4096]{1,0:T(8,128)(2,1)S(1)}, bf16[128,4096]{1,0:T(8,128)(2,1)}, u32[]{:S(2)}) copy-start(bf16[128,4096]{1,0:T(8,128)(2,1)} %param.11) | copy-start | bytes 3145732
  669.8 83.4 %copy-start.8 = (f32[128]{0:T(128)S(1)}, f32[128]{0:T(128)}, u32[]{:S(2)}) copy-start(f32[128]{0:T(128)} %param.10) | copy-start | bytes 1540
  669.9 190.2 %reduce-scatter.5.cloned.1.call-start = ((), (), s32[]{:S(2)}) async-start(), calls=%async_computation.6 | async-start | bytes 8912896 | tf_op jit(solution)/shard_map/reduce_scatter | solution.py:112
  759.9 100.2 %copy-start.1 = (bf16[3,4096,128]{2,1,0:T(8,128)(2,1)S(1)}, bf16[3,4096,128]{2,1,0:T(8,128)(2,1)}, u32[]{:S(2)}) copy-start(bf16[3,4096,128]{2,1,0:T(8,128)(2,1)} %param.7) | copy-start | bytes 9437188
Sparse Core Ops, SparseCore 0:
  9.1 127.2 all-gather.1
  670.0 83.2 reduce-scatter.2
  760.0 99.9 reduce-scatter.4
where the time goes:
time: 876 us; the launch traced here: 867 us
  matrix products  432 us (49%)
  waiting for transfers between devices  328 us (37%)
  other arithmetic  57.2 us (7%)
  blocking collectives  20 us (2%)
  between operations  14 us (2%)
  local copies, waits for them, and re-layouts  10.7 us (1%)
    dot_general x12, matrix products, three_pass(): jnp.einsum(form, left_high, right_low, preferred_element_type=jnp.float32)  142 us
    dot_general x12, matrix products, three_pass(): jnp.einsum(form, left_low, right_high, preferred_element_type=jnp.float32)  139 us
    dot_general x12, matrix products, three_pass(): jnp.einsum(form, left_high, right_high, preferred_element_type=jnp.float32)  138 us
    all_gather x1, waiting for transfers between devices, shards(): lax.all_gather(tokens, 'chan', axis=1, tiled=True)  129 us
    reduce_scatter x1, waiting for transfers between devices, shards(): lax.psum_scatter(partial_terms.astype(jnp.bfloat16), 'chan', scatter_dime...  100 us
    reduce_scatter x1, waiting for transfers between devices, shards(): lax.psum_scatter((partial_terms * norm_factor).astype(jnp.bfloat16), 'seq...  83.3 us
    convert_element_type x1, other arithmetic, shards(): (partial_terms * norm_factor).astype(jnp.bfloat16)  52.4 us
    all_to_all x1, blocking collectives, shards(): lax.all_to_all(signal[:, None, :], 'seq', split_axis=2, concat_axis=1, ti...  20 us
  transfers between devices with their start and end apart: 5, of which 5 were waited for; matrix products, arithmetic and copies ran while one was open for 0% of the time, Pallas kernels for 0%

commit v1 on v0

v1 whole, which is shorter than its diff:
```python
import math

import jax
import jax.numpy as jnp
import numpy as np
from jax import lax
from jax.experimental import pallas as pl
from jax.experimental.pallas import tpu as pltpu
from jax.sharding import PartitionSpec as P

MESH = pl.DeviceIdType.MESH
LANES = 128
SUB = 8
BF16 = jnp.bfloat16
F32 = jnp.float32


class Plan:
    def __init__(self, ns, nch, n_y, x_hi, tok, ds, ec):
        self.ns, self.nch, self.nz, self.n_y, self.x_hi = ns, nch, nch // 2, n_y, x_hi
        self.tok, self.half, self.ds, self.ec = tok, tok // 2, ds, ec
        self.cpd = SUB * ns
        self.d, self.e = nch * ds, nch * ec
        self.nhi = ns * tok // LANES
        self.ka = 2 * self.nhi
        self.nfft = 2 * ns * tok
        self.k1 = 2 * ns
        self.m = self.ka // self.k1
        self.k2 = self.m * LANES
        self.blocks = self.half // LANES
        self.rows = self.blocks * SUB
        self.piece = self.cpd // (2 * n_y)


def tables(plan):
    k1l, m, s = np.meshgrid(np.arange(2), np.arange(plan.m), np.arange(plan.ns), indexing="ij")
    ka = (2 * s + k1l + plan.k1 * m).reshape(-1).astype(np.int64)
    nhi = np.arange(plan.nhi, dtype=np.int64)
    lane = np.arange(LANES, dtype=np.int64)

    def angle(a, b, mod):
        return (a[:, None] * b[None, :] % mod) * (2.0 * math.pi / mod)

    left = angle(ka, nhi, plan.ka)
    f1 = np.concatenate([np.cos(left), -np.sin(left)], axis=0)
    g1 = np.concatenate([np.cos(left.T), -np.sin(left.T)], axis=1) / plan.nfft
    turn = angle(ka, lane, plan.nfft)
    tw = np.stack([np.cos(turn), -np.sin(turn)])
    right = angle(lane, lane, LANES)
    c, sn = np.cos(right), np.sin(right)
    f2 = np.block([[c, -sn], [sn, c]])
    g2 = np.block([[c, sn], [-sn, c]])
    order = np.zeros((plan.k2, plan.k2), np.float32)
    k2 = np.arange(plan.k2)
    order[k2, (k2 % plan.m) * LANES + k2 // plan.m] = 1.0
    as_bf16 = lambda a: jnp.asarray(a.astype(np.float32).astype(BF16))
    return (as_bf16(f1), as_bf16(g1), jnp.asarray(tw.astype(np.float32)), as_bf16(f2), as_bf16(g2), as_bf16(order))


def kernel(
    plan, tokens, in_w, spec, out_w, f1_h, g1_h, tw_h, f2_h, g2_h, ord_h, conv_w, skip_w, out,
    w_own, w_far, tok_v, acc, spec_v, ord_v, spec_s, spec_r, spec_f, proj_s, proj_r, proj_f,
    gate_f, gate_s, gate_r, gate_a, ow, o_acc, o_own, o_far, f1, g1, tw, f2, g2,
    load_sem, ring_send, ring_recv, ring2_send, ring2_recv, x_sem, w_send, w_recv,
    a2a_send, a2a_recv, ow_send, ow_recv, out_sem,
):
    ns, nz, nch, n_y, half, ds, ec = plan.ns, plan.nz, plan.nch, plan.n_y, plan.half, plan.ds, plan.ec
    s, c = lax.axis_index("seq"), lax.axis_index("chan")
    core, xh, y = lax.rem(s, 2), lax.rem(s // 2, plan.x_hi), s // (2 * plan.x_hi)
    xl, z = c // nz, lax.rem(c, nz)
    other = 1 - xl
    partner = other * nz + z

    def seq_of(y_, xh_, core_):
        return (y_ * plan.x_hi + xh_) * 2 + core_

    def remote(src, dst, ss, rs, seq, chan):
        return pltpu.make_async_remote_copy(
            src_ref=src, dst_ref=dst, send_sem=ss, recv_sem=rs,
            device_id={"seq": seq, "chan": chan}, device_id_type=MESH,
        )

    def arrived(ref, sem):
        pltpu.make_async_copy(ref, ref, sem).wait()

    loads = [
        (tokens.at[pl.ds(xl * half, half), :], tok_v.at[c]), (in_w, w_own), (spec, spec_v), (ord_h, ord_v),
        (f1_h, f1), (g1_h, g1), (tw_h, tw), (f2_h, f2), (g2_h, g2),
    ]
    loads = [pltpu.make_async_copy(a, b, load_sem.at[i]) for i, (a, b) in enumerate(loads)]

    me = xl * ns + s
    peers = 2 * ns
    bar = pltpu.get_barrier_semaphore()

    def greet_plane(d, carry):
        q = lax.rem(me + d, peers)
        pl.semaphore_signal(bar, inc=1, device_id={"seq": lax.rem(q, ns), "chan": (q // ns) * nz + z}, device_id_type=MESH)
        return carry

    def greet_line(d, carry):
        zz = lax.rem(z + d, nz)
        for g in range(2):
            pl.semaphore_signal(bar, inc=1, device_id={"seq": s, "chan": g * nz + zz}, device_id_type=MESH)
        return carry

    lax.fori_loop(1, peers, greet_plane, 0)
    lax.fori_loop(1, nz, greet_line, 0)
    for cp in loads:
        cp.start()
    pl.semaphore_wait(bar, peers - 1 + 2 * (nz - 1))

    hops = nz // 2
    reach = {(0, 0): hops, (1, 0): nz - 1 - hops, (0, 1): nz - 1 - hops, (1, 1): hops}

    def slot(grp, way, k):
        zz = lax.rem(z + nz - k, nz) if way == 0 else lax.rem(z + k, nz)
        return (xl if grp == 0 else other) * nz + zz

    def ring_copy(buf, send, recv, way, grp, k, src=None):
        to = lax.rem(z + 1, nz) if way == 0 else lax.rem(z + nz - 1, nz)
        at = slot(grp, way, k)
        return remote(buf.at[at] if src is None else src, buf.at[at], send.at[way, grp, k], recv.at[way, grp, k], s, xl * nz + to)

    sent = []

    def go(cp):
        cp.start()
        sent.append(cp)

    def ring_start(buf, send, recv, grp, src=None):
        for way in range(2):
            if reach[way, grp] > 0:
                go(ring_copy(buf, send, recv, way, grp, 0, src))

    def ring_step(buf, send, recv, grp, k):
        got = []
        for way in range(2):
            if k <= reach[way, grp]:
                at = slot(grp, way, k)
                arrived(buf.at[at], recv.at[way, grp, k - 1])
                if k < reach[way, grp]:
                    go(ring_copy(buf, send, recv, way, grp, k))
                got.append(at)
        return got

    mine = tokens.at[pl.ds(xl * half, half), :]
    x_copy = remote(tokens.at[pl.ds(other * half, half), :], tok_v.at[c], x_sem.at[0], x_sem.at[1], s, partner)
    x_copy.start()
    sent.append(x_copy)
    ring_start(tok_v, ring_send, ring_recv, 0, mine)

    quarter = plan.d // 4
    right_xh = lax.rem(xh + xl, plan.x_hi)
    left_xh = lax.rem(xh + plan.x_hi - 1 + xl, plan.x_hi)

    def w_rows(q):
        return pl.ds(pl.multiple_of(q * quarter, quarter), quarter)

    for i, xh_ in ((0, right_xh), (1, left_xh)):
        q = 2 * core + i
        go(remote(in_w.at[:, w_rows(q), :], w_far.at[:, w_rows(q), :], w_send.at[i], w_recv.at[i], seq_of(y, xh_, core), partner))

    loads[2].wait()
    loads[3].wait()

    step = min(plan.cpd * 2, 128)
    for p in range(2):
        for r0 in range(0, 2 * plan.cpd, step):
            turned = jnp.dot(spec_v[p, r0 : r0 + step, :], ord_v[...], preferred_element_type=F32).astype(BF16)
            for m in range(plan.m):
                spec_s[r0 // 16 : (r0 + step) // 16, p, m] = turned[:, m * LANES : (m + 1) * LANES].reshape(step // 16, 16, LANES)

    def send_spec(d, carry):
        q = lax.rem(s + d, ns)
        remote(spec_s.at[q], spec_r.at[s], a2a_send.at[0], a2a_recv.at[0], q, c).start()
        return carry

    lax.fori_loop(1, ns, send_spec, 0)
    spec_own = pltpu.make_async_copy(spec_s.at[s], spec_r.at[s], load_sem.at[9])
    spec_own.start()

    def project(grps, at, first=False):
        tk = tok_v[at]
        rows = pl.ds(pl.multiple_of(at * ds, ds), ds)
        for g in grps:
            w = w_own if g == 0 else w_far
            for p in range(3):
                part = lax.dot_general(w[p, rows, :], tk, (((0,), (1,)), ((), ())), preferred_element_type=F32)
                if first:
                    acc[g, p] = part
                else:
                    acc[g, p] = acc[g, p] + part

    loads[0].wait()
    loads[1].wait()
    project([0], c, True)
    arrived(tok_v.at[partner], x_sem.at[1])
    ring_start(tok_v, ring_send, ring_recv, 1)
    project([0], partner)
    far_ready = False
    for k in range(1, hops + 1):
        last = k == max(hops - 1, 1)
        got = ring_step(tok_v, ring_send, ring_recv, 0, k)
        if far_ready:
            for at in got:
                project([0, 1], at)
        elif not last:
            for at in got:
                project([0], at)
        more = ring_step(tok_v, ring_send, ring_recv, 1, k)
        if far_ready:
            for at in more:
                project([0, 1], at)
        elif not last:
            for at in more:
                project([0], at)
        else:
            side = pl.ds(pl.multiple_of(core * 2 * quarter, 2 * quarter), 2 * quarter)
            for i in range(2):
                arrived(w_far.at[:, w_rows(2 * core + i), :], w_recv.at[i])
            go(remote(w_far.at[:, side, :], w_far.at[:, side, :], w_send.at[2], w_recv.at[2], seq_of(y, xh, 1 - core), c))
            for at in got + more:
                project([0], at)
            away = pl.ds(pl.multiple_of((1 - core) * 2 * quarter, 2 * quarter), 2 * quarter)
            arrived(w_far.at[:, away, :], w_recv.at[2])
            far_ready = True
            project([1], c, True)
            project([1], partner)

            def catch_up(i, carry):
                for grp in range(2):
                    project([1], slot(grp, 1, i))
                return carry

            if k < hops:
                lax.fori_loop(1, k + 1, catch_up, 0)
                lax.fori_loop(nz - k, nz, catch_up, 0)
            else:
                lax.fori_loop(1, nz, catch_up, 0)

    row = pl.ds(pl.multiple_of((core * n_y + y) * plan.piece, plan.piece), plan.piece)

    def cols(b):
        return pl.ds(pl.multiple_of(b * ec, ec), ec)

    def ow_first(d, carry):
        to = lax.rem(c + d, nch)
        for g in range(2):
            remote(
                out_w.at[row, cols(g * nz + lax.rem(to, nz))], ow.at[c, row, g * ec : (g + 1) * ec],
                ow_send.at[0], ow_recv.at[0], s, to,
            ).start()
        return carry

    ow_own = [
        pltpu.make_async_copy(out_w.at[row, cols(g * nz + z)], ow.at[c, row, g * ec : (g + 1) * ec], load_sem.at[10 + g])
        for g in range(2)
    ]

    for g in range(2):
        q0 = jnp.where(g == 0, xl, other) * ns
        for p in range(3):
            for j in range(plan.blocks // 2):
                pair = [
                    acc[g, p, :, (2 * j + i) * LANES : (2 * j + i + 1) * LANES].reshape(ns, SUB, LANES) for i in range(2)
                ]
                proj_s[pl.ds(q0, ns), p, j] = jnp.concatenate(pair, axis=1).astype(BF16)

    here = 2 * s + xl

    def send_proj(d, carry):
        q = lax.rem(me + d, peers)
        remote(proj_s.at[q], proj_r.at[here], a2a_send.at[1], a2a_recv.at[1], lax.rem(q, ns), (q // ns) * nz + z).start()
        return carry

    lax.fori_loop(1, peers, send_proj, 0)
    proj_own = pltpu.make_async_copy(proj_s.at[me], proj_r.at[here], load_sem.at[12])
    proj_own.start()
    lax.fori_loop(1, nch, ow_first, 0)
    for cp in ow_own:
        cp.start()

    spec_own.wait()
    arrived(spec_r.at[0 : ns - 1], a2a_recv.at[0])

    def lay(i, carry):
        for p in range(2):
            for m in range(plan.m):
                spec_f[p, pl.ds(pl.multiple_of((m * ns + i) * 16, 16), 16), :] = spec_r[i, p, m].astype(F32)
        return carry

    lax.fori_loop(0, ns, lay, 0)
    for cp in loads[4:]:
        cp.wait()

    proj_own.wait()
    arrived(proj_r.at[0 : peers - 1], a2a_recv.at[1])
    for cp in ow_own:
        cp.wait()
    arrived(ow.at[0 : nch - 1, row, :], ow_recv.at[0])
    for dy in range(1, n_y):
        go(remote(ow.at[:, row, :], ow.at[:, row, :], ow_send.at[dy], ow_recv.at[dy], seq_of(lax.rem(y + dy, n_y), xh, core), c))

    for p in range(3):
        proj_f[p] = proj_r[:, p].astype(F32).reshape(plan.nhi * SUB, LANES)

    lane = lax.broadcasted_iota(jnp.int32, (plan.nhi, LANES), 1)
    posn = lane + LANES * lax.broadcasted_iota(jnp.int32, (plan.nhi, LANES), 0)

    def behind(x, by):
        turned = pltpu.roll(x, by, 1)
        both = jnp.where(lane < by, pltpu.roll(turned, 1, 0), turned)
        return jnp.where(posn < by, 0.0, both)

    def transform(ch, carry):
        chan = s * SUB + ch
        parts = []
        for p in range(3):
            x = proj_f[p, pl.ds(ch, plan.nhi, stride=SUB), :]
            f = conv_w[0, p, chan] * x
            for j in range(1, 3):
                f = f + conv_w[j, p, chan] * behind(x, j)
            parts.append(f)
        query, signal = parts[0], (parts[1] * parts[2]).astype(BF16)
        a = jnp.dot(f1[...], signal, preferred_element_type=F32)
        ar, ai = a[: plan.ka], a[plan.ka :]
        tr, ti = tw[0], tw[1]
        yy = jnp.concatenate([(ar * tr - ai * ti).astype(BF16), (ar * ti + ai * tr).astype(BF16)], axis=1)
        zz = jnp.dot(yy, f2[...], preferred_element_type=F32)
        zr, zi = zz[:, :LANES], zz[:, LANES:]
        h = []
        for p in range(2):
            h.append(jnp.concatenate(
                [spec_f[p, pl.ds(2 * ch + k, plan.m * ns, stride=16), :] for k in range(2)], axis=0))
        pp = jnp.concatenate([(zr * h[0] - zi * h[1]).astype(BF16), (zr * h[1] + zi * h[0]).astype(BF16)], axis=1)
        u = jnp.dot(pp, g2[...], preferred_element_type=F32)
        ur, ui = u[:, :LANES], u[:, LANES:]
        v = jnp.concatenate([(ur * tr + ui * ti).astype(BF16), (ui * tr - ur * ti).astype(BF16)], axis=0)
        longconv = jnp.dot(g1[...], v, preferred_element_type=F32)
        gate_f[pl.ds(ch, plan.nhi, stride=SUB), :] = query * (longconv + skip_w[chan] * signal.astype(F32))
        return carry

    lax.fori_loop(0, SUB, transform, 0, unroll=2)
    gate_s[...] = gate_f[...].astype(BF16).reshape(peers, plan.rows, LANES)

    def send_gate(d, carry):
        q = lax.rem(here + d, peers)
        remote(gate_s.at[q], gate_r.at[me], a2a_send.at[2], a2a_recv.at[2], q // 2, lax.rem(q, 2) * nz + z).start()
        return carry

    lax.fori_loop(1, peers, send_gate, 0)
    gate_own = pltpu.make_async_copy(gate_s.at[here], gate_r.at[me], load_sem.at[13])
    gate_own.start()
    for dy in range(1, n_y):
        yy = lax.rem(y + n_y - dy, n_y)
        piece = pl.ds(pl.multiple_of((core * n_y + yy) * plan.piece, plan.piece), plan.piece)
        arrived(ow.at[:, piece, :], ow_recv.at[dy])
    wide = plan.piece * n_y
    side = pl.ds(pl.multiple_of(core * wide, wide), wide)
    go(remote(ow.at[:, side, :], ow.at[:, side, :], ow_send.at[n_y], ow_recv.at[n_y], seq_of(y, xh, 1 - core), c))

    gate_own.wait()
    arrived(gate_r.at[0 : peers - 1], a2a_recv.at[2])
    for grp in range(2):
        g = xl if grp == 0 else other
        for j in range(plan.blocks // 2):
            pair = gate_r[pl.ds(g * ns, ns), 16 * j : 16 * (j + 1), :].astype(F32)
            for i in range(2):
                block = pair[:, SUB * i : SUB * (i + 1), :].reshape(plan.cpd, LANES)
                at = (2 * j + i) * LANES
                gate_a[g * nz + z, at : at + LANES, :] = block.T.astype(BF16)
        ring_start(gate_a, ring2_send, ring2_recv, grp)
    away = pl.ds(pl.multiple_of((1 - core) * wide, wide), wide)
    arrived(ow.at[:, away, :], ow_recv.at[n_y])

    def mix(at):
        o_acc[...] = o_acc[...] + jnp.dot(gate_a[at], ow[at], preferred_element_type=F32)

    o_acc[...] = jnp.dot(gate_a[c], ow[c], preferred_element_type=F32)
    mix(partner)
    for k in range(1, hops + 1):
        for grp in range(2):
            for at in ring_step(gate_a, ring2_send, ring2_recv, grp, k):
                mix(at)

    mixed = [o_acc[:, g * ec : (g + 1) * ec].astype(BF16) for g in range(2)]
    o_far[...] = jnp.where(xl == 0, mixed[1], mixed[0])
    mine = pl.ds(pl.multiple_of(xl * half, half), half)
    theirs = pl.ds(pl.multiple_of(other * half, half), half)
    go(remote(o_far, out.at[mine, :], out_sem.at[0], out_sem.at[1], s, partner))
    o_own[...] = jnp.where(xl == 0, mixed[0], mixed[1])
    keep = pltpu.make_async_copy(o_own, out.at[mine, :], out_sem.at[2])
    keep.start()

    for cp in sent:
        cp.wait_send()
    arrived(spec_s.at[0 : ns - 1], a2a_send.at[0])
    arrived(proj_s.at[0 : peers - 1], a2a_send.at[1])
    arrived(gate_s.at[0 : peers - 1], a2a_send.at[2])
    arrived(ow.at[0 : nch - 1, row, :], ow_send.at[0])
    keep.wait()
    arrived(out.at[theirs, :], out_sem.at[1])


def make(plan):
    consts = tables(plan)

    def shards(tokens, in_weight, conv_weight, spectrum, skip, out_weight):
        spec = spectrum.reshape(2, 2 * plan.cpd, plan.k2).astype(BF16)
        ns, peers, cpd = plan.ns, 2 * plan.ns, plan.cpd
        hops = plan.nz // 2
        vm = pltpu.VMEM
        dma = pltpu.SemaphoreType.DMA
        anywhere = pl.BlockSpec(memory_space=pl.ANY)
        scalars = pl.BlockSpec(memory_space=pltpu.SMEM)
        return pl.pallas_call(
            lambda *refs: kernel(plan, *refs),
            out_shape=jax.ShapeDtypeStruct((plan.tok, plan.ec), BF16),
            in_specs=[anywhere] * 10 + [scalars] * 2,
            out_specs=anywhere,
            scratch_shapes=[
                vm((3, plan.d, cpd), BF16), vm((3, plan.d, cpd), BF16),
                vm((plan.nch, plan.half, plan.ds), BF16),
                vm((2, 3, cpd, plan.half), F32),
                vm((2, 2 * cpd, plan.k2), BF16), vm((plan.k2, plan.k2), BF16),
                vm((ns, 2, plan.m, 16, LANES), BF16), vm((ns, 2, plan.m, 16, LANES), BF16),
                vm((2, plan.m * ns * 16, LANES), F32),
                vm((peers, 3, plan.blocks // 2, 16, LANES), BF16),
                vm((peers, 3, plan.blocks // 2, 16, LANES), BF16),
                vm((3, plan.nhi * SUB, LANES), F32),
                vm((plan.nhi * SUB, LANES), F32),
                vm((peers, plan.rows, LANES), BF16), vm((peers, plan.rows, LANES), BF16),
                vm((plan.nch, plan.half, cpd), BF16),
                vm((plan.nch, cpd, 2 * plan.ec), BF16),
                vm((plan.half, 2 * plan.ec), F32),
                vm((plan.half, plan.ec), BF16), vm((plan.half, plan.ec), BF16),
                vm((2 * plan.ka, plan.nhi), BF16), vm((plan.nhi, 2 * plan.ka), BF16),
                vm((2, plan.ka, LANES), F32),
                vm((2 * LANES, 2 * LANES), BF16), vm((2 * LANES, 2 * LANES), BF16),
                dma((14,)), dma((2, 2, hops)), dma((2, 2, hops)), dma((2, 2, hops)), dma((2, 2, hops)),
                dma((2,)), dma((3,)), dma((3,)), dma((3,)), dma((3,)),
                dma((plan.n_y + 1,)), dma((plan.n_y + 1,)), dma((3,)),
            ],
            compiler_params=pltpu.CompilerParams(
                collective_id=0, has_side_effects=True, vmem_limit_bytes=56 * 1024 * 1024
            ),
            name="hyena",
        )(tokens, in_weight, spec, out_weight, *consts, conv_weight, skip)

    return shards


def on_mesh(mesh, plan):
    placed = (
        P("seq", "chan"),
        P(None, None, "chan"),
        P(None, None, "chan"),
        P(None, "chan", "seq", None),
        P("chan"),
        P("chan", None),
    )
    return jax.shard_map(make(plan), mesh=mesh, in_specs=placed, out_specs=P("seq", "chan"), check_vma=False)


def solution(mesh):
    return on_mesh(mesh, Plan(ns=16, nch=16, n_y=4, x_hi=2, tok=1024, ds=256, ec=256))
```

time: 876 us -> 125 us (0.14)
  matrix products: 432 us -> 0 us
  waiting for transfers between devices: 328 us -> 0 us
  Pallas kernels: 0 us -> 119 us
  other arithmetic: 57.2 us -> 2.31 us
  blocking collectives: 20 us -> 0 us
  between operations: 14 us -> 0.01 us
    dot_general x38 -> x0, matrix products: 432 us -> none  [the longest x12 142 us: three_pass(): jnp.einsum(form, left_high, right_low, preferred_element_type=jnp.float32)]
    reduce_scatter x2 -> x0, waiting for transfers between devices: 183 us -> none  [the longest x1 100 us: shards(): lax.psum_scatter(partial_terms.astype(jnp.bfloat16), 'chan', scatter_dime...]
    all_gather x1 -> x0, waiting for transfers between devices: 129 us -> none  [shards(): lax.all_gather(tokens, 'chan', axis=1, tiled=True)]
    pallas_call x0 -> x1, Pallas kernels: none -> 119 us  [shards(): pl.pallas_call(lambda *refs: kernel(plan, *refs), out_shape=jax.ShapeDtyp...]
    convert_element_type x6 -> x1, other arithmetic: 53.5 us -> 2.31 us  [shards(): spec = spectrum.reshape(2, 2 * plan.cpd, plan.k2).astype(BF16)]
    all_to_all x1 -> x0, blocking collectives: 20 us -> none  [shards(): lax.all_to_all(signal[:, None, :], 'seq', split_axis=2, concat_axis=1, ti...]
    all_to_all x1 -> x0, waiting for transfers between devices: 13.9 us -> none  [shards(): lax.all_to_all(stacked.astype(jnp.bfloat16), 'seq', split_axis=2, concat_...]
  transfers between devices with their start and end apart: 5 -> 0, of which waited for: 5 -> 0; matrix products, arithmetic and copies ran while one was open for 0% -> 0% of each run, Pallas kernels for 0% -> 0%
where the time goes in v1:
time: 125 us
  Pallas kernels  119 us (95%)
  local copies, waits for them, and re-layouts  3.11 us (2%)
  other arithmetic  2.31 us (2%)
    pallas_call x1, Pallas kernels, shards(): pl.pallas_call(lambda *refs: kernel(plan, *refs), out_shape=jax.ShapeDtyp...  119 us

profile of v1, /device:TPU:2, one launch (start us, length us, event | category | flops | bytes accessed | tf_op | source)
XLA Modules:
  0.0 124.6 jit_solution(16012336548727114609)
XLA Ops:
  0.0 2.3 %convert_element_type.5 = bf16[2,128,2,1024]{3,2,1,0:T(2,128)(2,1)S(1)} convert(f32[2,128,2,1024]{3,2,1,0:T(2,128)} %param.15) | non-fusion elementwise | flops 524288 | bytes 3145728 | tf_op jit(solution)/shard_map/convert_element_type | solution.py:410
  2.3 1.2 convert_element_type.6.refs_2_
  3.6 119.2 %hyena.1 = bf16[1024,256]{1,0:T(8,128)(2,1)} custom-call(bf16[1024,256]{1,0:T(8,128)(2,1)} %refs_0_.1, bf16[3,4096,128]{2,1,0:T(8,128)(2,1)} %refs_1_.1, bf16[2,256,1024]{2,1,0:T(8,128)(2,1)} %convert_element_type.6.refs_2_, bf16[128,4096]{1,0:T(8,128)(2,1)} %refs_3_.1, bf16[512,128]{1,0:T(8,128)(2,1)} %constant.12.clone.refs_4_, ...), custom_call_target="tpu_custom_call" | custom-call | tf_op jit(solution)/shard_map/hyena/pallas_call | solution.py:417
  122.7 1.9 %copy.14 = bf16[1024,256]{1,0:T(8,128)(2,1)} copy(bf16[1024,256]{1,0:T(8,128)(2,1)} %hyena.1) | data formatting | bytes 1048576

commit v2 on v1

v2 whole, which is shorter than its diff:
```python
import math

import jax
import jax.numpy as jnp
import numpy as np
from jax import lax
from jax.experimental import pallas as pl
from jax.experimental.pallas import tpu as pltpu
from jax.sharding import PartitionSpec as P

MESH = pl.DeviceIdType.MESH
LANES = 128
SUB = 8
BF16 = jnp.bfloat16
F32 = jnp.float32


class Plan:
    def __init__(self, ns, nch, n_y, x_hi, tok, ds, ec):
        self.ns, self.nch, self.nz, self.n_y, self.x_hi = ns, nch, nch // 2, n_y, x_hi
        self.tok, self.half, self.ds, self.ec = tok, tok // 2, ds, ec
        self.cpd = SUB * ns
        self.d, self.e = nch * ds, nch * ec
        self.nhi = ns * tok // LANES
        self.ka = 2 * self.nhi
        self.nfft = 2 * ns * tok
        self.k1 = 2 * ns
        self.m = self.ka // self.k1
        self.k2 = self.m * LANES
        self.blocks = self.half // LANES
        self.rows = self.blocks * SUB
        self.piece = self.cpd // (2 * n_y)


def tables(plan):
    m, s, k1l = np.meshgrid(np.arange(plan.m), np.arange(plan.ns), np.arange(2), indexing="ij")
    ka = (2 * s + k1l + plan.k1 * m).reshape(-1).astype(np.int64)
    nhi = np.arange(plan.nhi, dtype=np.int64)
    lane = np.arange(LANES, dtype=np.int64)

    def angle(a, b, mod):
        return (a[:, None] * b[None, :] % mod) * (2.0 * math.pi / mod)

    left = angle(ka, nhi, plan.ka)
    f1 = np.concatenate([np.cos(left), -np.sin(left)], axis=0)
    g1 = np.concatenate([np.cos(left.T), -np.sin(left.T)], axis=1) / plan.nfft
    turn = angle(ka, lane, plan.nfft)
    tw = np.stack([np.cos(turn), -np.sin(turn)])
    right = angle(lane, lane, LANES)
    c, sn = np.cos(right), np.sin(right)
    f2 = np.block([[c, -sn], [sn, c]])
    g2 = np.block([[c, sn], [-sn, c]])
    order = np.zeros((plan.k2, plan.k2), np.float32)
    k2 = np.arange(plan.k2)
    order[k2, (k2 % plan.m) * LANES + k2 // plan.m] = 1.0
    as_bf16 = lambda a: jnp.asarray(a.astype(np.float32).astype(BF16))
    return (as_bf16(f1), as_bf16(g1), jnp.asarray(tw.astype(np.float32)), as_bf16(f2), as_bf16(g2), as_bf16(order))


def kernel(
    plan, tokens, in_w, spec, out_w, f1_h, g1_h, tw_h, f2_h, g2_h, ord_h, conv_w, skip_w, out,
    w_all, tok_v, acc, spec_v, ord_v, spec_s, spec_r, spec_f, proj_s, proj_r, proj_f,
    gate_f, gate_s, gate_r, gate_a, ow, o_acc, o_own, o_far, f1, g1, tw, f2, g2,
    load_sem, ring_send, ring_recv, ring2_send, ring2_recv, x_send, x_recv, w_send, w_recv,
    a2a_send, a2a_recv, ow_send, ow_recv, out_send, out_recv,
):
    ns, nz, nch, n_y, half, ds, ec, cpd = plan.ns, plan.nz, plan.nch, plan.n_y, plan.half, plan.ds, plan.ec, plan.cpd
    s, c = lax.axis_index("seq"), lax.axis_index("chan")
    core, xh, y = lax.rem(s, 2), lax.rem(s // 2, plan.x_hi), s // (2 * plan.x_hi)
    xl, z = c // nz, lax.rem(c, nz)
    other = 1 - xl
    partner = other * nz + z
    me, here, peers = xl * ns + s, 2 * s + xl, 2 * ns
    hops = nz // 2
    part = half // 2
    wide = 3 * cpd

    def seq_of(y_, xh_, core_):
        return (y_ * plan.x_hi + xh_) * 2 + core_

    def remote(src, dst, ss, rs, seq, chan):
        return pltpu.make_async_remote_copy(
            src_ref=src, dst_ref=dst, send_sem=ss, recv_sem=rs,
            device_id={"seq": seq, "chan": chan}, device_id_type=MESH,
        )

    def arrived(ref, sem):
        pltpu.make_async_copy(ref, ref, sem).wait()

    def place(grp, off):
        k = min(off, nz - off) if isinstance(off, int) else jnp.minimum(off, nz - off)
        return 4 * k - 2 + 2 * ((nz - 1 - off) // hops) + grp

    def origin(side, at):
        grp, off = next((g, o) for g in range(2) for o in range(nz) if place(g, o) == at)
        return (side if grp == 0 else 1 - side) * nz + lax.rem(z + off, nz)

    def rows_of(block):
        return pl.ds(pl.multiple_of(block * ds, ds), ds)

    def start_weights():
        for at in range(nch):
            rows = rows_of(origin(xl, at))
            for p in range(3):
                pltpu.make_async_copy(
                    in_w.at[p, rows, :], w_all.at[at * ds : (at + 1) * ds, p * cpd : (p + 1) * cpd], load_sem.at[1]
                ).start()

    loads = [pltpu.make_async_copy(tokens.at[pl.ds(xl * half, half), :], tok_v.at[:, 0:ds], load_sem.at[0])]
    loads += [pltpu.make_async_copy(a, b, load_sem.at[2 + i]) for i, (a, b) in enumerate(
        [(ord_h, ord_v), (f1_h, f1), (g1_h, g1), (tw_h, tw), (f2_h, f2), (g2_h, g2)])]
    spec_loads = [
        pltpu.make_async_copy(spec.at[p, :, k, :], spec_v.at[p, k], load_sem.at[8 + 2 * p + k])
        for p in range(2) for k in range(2)
    ]

    bar = pltpu.get_barrier_semaphore()

    def greet_plane(d, carry):
        q = lax.rem(me + d, peers)
        pl.semaphore_signal(bar, inc=1, device_id={"seq": lax.rem(q, ns), "chan": (q // ns) * nz + z}, device_id_type=MESH)
        return carry

    def greet_line(d, carry):
        pl.semaphore_signal(bar, inc=1, device_id={"seq": s, "chan": xl * nz + lax.rem(z + d, nz)}, device_id_type=MESH)
        return carry

    lax.fori_loop(1, peers, greet_plane, 0)
    lax.fori_loop(1, nz, greet_line, 0)
    for cp in loads[:2] + spec_loads:
        cp.start()
    start_weights()
    for cp in loads[2:]:
        cp.start()
    pl.semaphore_wait(bar, peers - 1 + nz - 1)

    reach = {(0, 0): hops, (1, 0): nz - 1 - hops, (0, 1): nz - 1 - hops, (1, 1): hops}
    sent = []

    def go(cp):
        cp.start()
        sent.append(cp)

    class Ring:
        def __init__(self, buf, width, send, recv):
            self.buf, self.width, self.send, self.recv = buf, width, send, recv

        def item(self, r, way, grp, k):
            at = place(grp, (nz - k if way == 0 else k) % nz)
            return self.buf.at[r * part : (r + 1) * part, at * self.width : (at + 1) * self.width]

        def hand_on(self, r, way, grp, k, src=None):
            to = lax.rem(z + 1, nz) if way == 0 else lax.rem(z + nz - 1, nz)
            go(remote(
                self.item(r, way, grp, k) if src is None else src, self.item(r, way, grp, k + 1),
                self.send.at[r, way, grp, k], self.recv.at[r, way, grp, k], s, xl * nz + to,
            ))

        def begin(self, r, grp, src=None):
            for way in range(2):
                if reach[way, grp] > 0:
                    self.hand_on(r, way, grp, 0, src)

        def step(self, r, k):
            for grp in range(2):
                for way in range(2):
                    if k <= reach[way, grp]:
                        arrived(self.item(r, way, grp, k), self.recv.at[r, way, grp, k - 1])
                        if k < reach[way, grp]:
                            self.hand_on(r, way, grp, k)

    def token_rows(side, r):
        return tokens.at[pl.ds(pl.multiple_of(side * half + r * part, part), part), :]

    ring = Ring(tok_v, ds, ring_send, ring_recv)
    far_home = tok_v.at[:, ds : 2 * ds]

    def swap(r):
        go(remote(token_rows(other, r), far_home.at[r * part : (r + 1) * part, :], x_send.at[r], x_recv.at[r], s, partner))

    swap(0)
    ring.begin(0, 0, token_rows(xl, 0))
    swap(1)

    quarter = nch // 4

    def far_rows(i):
        q = (2 * core + i) * quarter * ds
        return pl.ds(pl.multiple_of(q, quarter * ds), quarter * ds)

    for i, xh_ in ((0, lax.rem(xh + xl, plan.x_hi)), (1, lax.rem(xh + plan.x_hi - 1 + xl, plan.x_hi))):
        for j in range(quarter):
            first, second = origin(other, i * quarter + j), origin(other, (2 + i) * quarter + j)
            rows = rows_of(first + core * (second - first))
            to = pl.ds(pl.multiple_of((2 * core + i) * quarter * ds + j * ds, ds), ds)
            for p in range(3):
                remote(
                    in_w.at[p, rows, :], w_all.at[to, wide + p * cpd : wide + (p + 1) * cpd],
                    w_send.at[i], w_recv.at[i], seq_of(y, xh_, core), partner,
                ).start()

    row = pl.ds(pl.multiple_of((core * n_y + y) * plan.piece, plan.piece), plan.piece)
    if plan.x_hi == 2:
        sides = [(xh, pl.ds(pl.multiple_of(xh * ec, ec), ec))]
    else:
        sides = [(0, pl.ds(0, ec)), (1, pl.ds(ec, ec))]

    def out_cols(g, zz):
        return pl.ds(pl.multiple_of((g * nz + zz) * ec, ec), ec)

    def ow_first(d, carry):
        zz = lax.rem(z + d, nz)
        at = place(0, nz - d) // 2
        for g, to in sides:
            remote(out_w.at[row, out_cols(g, zz)], ow.at[at, 0, row, to], ow_send.at[0], ow_recv.at[0], s, xl * nz + zz).start()
        return carry

    lax.fori_loop(1, nz, ow_first, 0)
    ow_own = [
        pltpu.make_async_copy(out_w.at[row, out_cols(g, z)], ow.at[0, 0, row, to], load_sem.at[12 + i])
        for i, (g, to) in enumerate(sides)
    ]
    for cp in ow_own:
        cp.start()

    arrived(far_home.at[0:part, :], x_recv.at[0])
    ring.begin(0, 1)

    loads[1].wait()
    for p in range(2):
        turned = []
        for k in range(2):
            spec_loads[2 * p + k].wait()
            turned.append(jnp.dot(spec_v[p, k].astype(BF16), ord_v[...], preferred_element_type=F32))
        for m in range(plan.m):
            pair = [t[:, m * LANES : (m + 1) * LANES].reshape(ns, SUB, LANES) for t in turned]
            spec_s[:, p, m] = jnp.concatenate(pair, axis=1).astype(BF16)
    spec_own = pltpu.make_async_copy(spec_s.at[s], spec_r.at[s], load_sem.at[14])
    spec_own.start()

    def send_spec(d, carry):
        q = lax.rem(s + d, ns)
        remote(spec_s.at[q], spec_r.at[s], a2a_send.at[0], a2a_recv.at[0], q, c).start()
        return carry

    def pack(value, r, g, p):
        pair = [value[i * LANES : (i + 1) * LANES, :].T.reshape(ns, SUB, LANES) for i in range(2)]
        at = xl if g == 0 else other
        proj_s[pl.ds(at * ns, ns), r, p] = jnp.concatenate(pair, axis=1).astype(BF16)

    def send_proj(r, g):
        def one(d, carry):
            q = lax.rem(s + d, ns)
            remote(
                proj_s.at[(xl if g == 0 else other) * ns + q, r], proj_r.at[here, r], a2a_send.at[1 + r], a2a_recv.at[1 + r],
                q, c if g == 0 else partner,
            ).start()
            return carry

        lax.fori_loop(1 - g, ns, one, 0)
        if g == 0:
            pltpu.make_async_copy(proj_s.at[me, r], proj_r.at[here, r], load_sem.at[15 + r]).start()

    def project(r, g):
        rows = slice(r * part, (r + 1) * part)
        value = jnp.dot(tok_v[rows, :], w_all[:, g * wide : (g + 1) * wide], preferred_element_type=F32)
        for p in range(3):
            pack(value[:, p * cpd : (p + 1) * cpd], r, g, p)
        send_proj(r, g)

    def ow_second():
        for cp in ow_own:
            cp.wait()
        mine = ow.at[:, 0, row, sides[0][1]] if plan.x_hi == 2 else ow.at[:, 0, row, :]
        arrived(mine.at[0 : nz - 1], ow_recv.at[0])
        far = ow.at[:, 1, row, sides[0][1]] if plan.x_hi == 2 else ow.at[:, 1, row, :]
        go(remote(mine, far, ow_send.at[1], ow_recv.at[1], s, partner))
        if plan.x_hi == 2:
            go(remote(mine, mine, ow_send.at[2], ow_recv.at[2], seq_of(y, 1 - xh, core), c))
            go(remote(mine, far, ow_send.at[3], ow_recv.at[3], seq_of(y, 1 - xh, core), partner))

    def ow_third():
        if plan.x_hi == 2:
            away = pl.ds(pl.multiple_of((1 - xh) * ec, ec), ec)
            arrived(ow.at[:, 1, row, sides[0][1]], ow_recv.at[1])
            arrived(ow.at[:, 0, row, away], ow_recv.at[2])
            arrived(ow.at[:, 1, row, away], ow_recv.at[3])
        else:
            arrived(ow.at[:, 1, row, :], ow_recv.at[1])
        for dy in range(1, n_y):
            go(remote(ow.at[:, :, row, :], ow.at[:, :, row, :], ow_send.at[3 + dy], ow_recv.at[3 + dy],
                      seq_of(lax.rem(y + dy, n_y), xh, core), c))

    half_ow = n_y * plan.piece

    def ow_fourth():
        for dy in range(1, n_y):
            yy = lax.rem(y + n_y - dy, n_y)
            piece = pl.ds(pl.multiple_of((core * n_y + yy) * plan.piece, plan.piece), plan.piece)
            arrived(ow.at[:, :, piece, :], ow_recv.at[3 + dy])
        side = pl.ds(pl.multiple_of(core * half_ow, half_ow), half_ow)
        go(remote(ow.at[:, :, side, :], ow.at[:, :, side, :], ow_send.at[3 + n_y], ow_recv.at[3 + n_y], seq_of(y, xh, 1 - core), c))

    def ow_last():
        away = pl.ds(pl.multiple_of((1 - core) * half_ow, half_ow), half_ow)
        arrived(ow.at[:, :, away, :], ow_recv.at[3 + n_y])

    def far_pass():
        for i in range(2):
            arrived(w_all.at[far_rows(i), wide : 2 * wide], w_recv.at[i])
        side = pl.ds(pl.multiple_of(core * 2 * quarter * ds, 2 * quarter * ds), 2 * quarter * ds)
        mine = w_all.at[side, wide : 2 * wide]
        go(remote(mine, mine, w_send.at[2], w_recv.at[2], seq_of(y, xh, 1 - core), c))

    def far_wait():
        away = pl.ds(pl.multiple_of((1 - core) * 2 * quarter * ds, 2 * quarter * ds), 2 * quarter * ds)
        arrived(w_all.at[away, wide : 2 * wide], w_recv.at[2])

    for k in range(1, hops + 1):
        ring.step(0, k)
        if k == max(hops - 1, 1):
            arrived(far_home.at[part : 2 * part, :], x_recv.at[1])
            ring.begin(1, 0, token_rows(xl, 1))
            ring.begin(1, 1)
        if k == 1:
            ow_second()
    loads[0].wait()
    arrived(w_all.at[:, 0:wide], load_sem.at[1])
    ow_third()
    project(0, 0)
    for k in range(1, hops):
        ring.step(1, k)
        if k == 1:
            far_pass()
            lax.fori_loop(1, ns, send_spec, 0)
        if k == 2:
            far_wait()
            project(0, 1)
    if hops < 2:
        far_pass()
        lax.fori_loop(1, ns, send_spec, 0)
    if hops < 3:
        far_wait()
        project(0, 1)
    ow_fourth()
    bulk = (nch - 2) * ds
    rows = slice(part, 2 * part)
    for g in range(2):
        for p in range(3):
            at = g * wide + p * cpd
            if (at // cpd) % 2 == 0:
                acc[:, at : at + 2 * cpd] = jnp.dot(
                    tok_v[rows, 0:bulk], w_all[0:bulk, at : at + 2 * cpd], preferred_element_type=F32)
    ring.step(1, hops)
    rest = acc[...] + jnp.dot(tok_v[rows, bulk:], w_all[bulk:, :], preferred_element_type=F32)
    for g in range(2):
        for p in range(3):
            at = g * wide + p * cpd
            pack(rest[:, at : at + cpd], 1, g, p)
        send_proj(1, g)

    spec_own.wait()
    arrived(spec_r.at[0 : ns - 1], a2a_recv.at[0])

    def lay(i, carry):
        for p in range(2):
            for m in range(plan.m):
                spec_f[p, pl.ds(pl.multiple_of((m * ns + i) * 16, 16), 16), :] = spec_r[i, p, m].astype(F32)
        return carry

    lax.fori_loop(0, ns, lay, 0)
    for cp in loads[2:]:
        cp.wait()
    for r in range(2):
        arrived(proj_r.at[here, r], load_sem.at[15 + r])
        arrived(proj_r.at[0 : peers - 1, r], a2a_recv.at[1 + r])
    for p in range(3):
        proj_f[p] = proj_r[:, :, p].astype(F32).reshape(plan.nhi * SUB, LANES)

    lane = lax.broadcasted_iota(jnp.int32, (plan.nhi, LANES), 1)
    posn = lane + LANES * lax.broadcasted_iota(jnp.int32, (plan.nhi, LANES), 0)

    def behind(x, by):
        turned = pltpu.roll(x, by, 1)
        both = jnp.where(lane < by, pltpu.roll(turned, 1, 0), turned)
        return jnp.where(posn < by, 0.0, both)

    def transform(ch, carry):
        chan = s * SUB + ch
        parts = []
        for p in range(3):
            x = proj_f[p, pl.ds(ch, plan.nhi, stride=SUB), :]
            f = conv_w[0, p, chan] * x
            for j in range(1, 3):
                f = f + conv_w[j, p, chan] * behind(x, j)
            parts.append(f)
        query, signal = parts[0], (parts[1] * parts[2]).astype(BF16)
        a = jnp.dot(f1[...], signal, preferred_element_type=F32)
        ar, ai = a[: plan.ka], a[plan.ka :]
        tr, ti = tw[0], tw[1]
        yy = jnp.concatenate([(ar * tr - ai * ti).astype(BF16), (ar * ti + ai * tr).astype(BF16)], axis=1)
        zz = jnp.dot(yy, f2[...], preferred_element_type=F32)
        zr, zi = zz[:, :LANES], zz[:, LANES:]
        hr, hi = (spec_f[p, pl.ds(ch, plan.ka, stride=SUB), :] for p in range(2))
        pp = jnp.concatenate([(zr * hr - zi * hi).astype(BF16), (zr * hi + zi * hr).astype(BF16)], axis=1)
        u = jnp.dot(pp, g2[...], preferred_element_type=F32)
        ur, ui = u[:, :LANES], u[:, LANES:]
        v = jnp.concatenate([(ur * tr + ui * ti).astype(BF16), (ui * tr - ur * ti).astype(BF16)], axis=0)
        longconv = jnp.dot(g1[...], v, preferred_element_type=F32)
        gate_f[pl.ds(ch, plan.nhi, stride=SUB), :] = query * (longconv + skip_w[chan] * signal.astype(F32))
        return carry

    lax.fori_loop(0, SUB, transform, 0, unroll=True)
    gate_s[...] = gate_f[...].astype(BF16).reshape(peers, plan.rows, LANES)

    def send_gate(d, carry):
        q = lax.rem(here + d, peers)
        remote(gate_s.at[q], gate_r.at[me], a2a_send.at[3], a2a_recv.at[3], q // 2, lax.rem(q, 2) * nz + z).start()
        return carry

    lax.fori_loop(1, peers, send_gate, 0)
    gate_own = pltpu.make_async_copy(gate_s.at[here], gate_r.at[me], load_sem.at[17])
    gate_own.start()
    gate_own.wait()
    arrived(gate_r.at[0 : peers - 1], a2a_recv.at[3])

    ring2 = Ring(gate_a, cpd, ring2_send, ring2_recv)

    def repack(r):
        for grp in range(2):
            pair = gate_r[pl.ds((xl if grp == 0 else other) * ns, ns), 16 * r : 16 * (r + 1), :].astype(F32)
            for i in range(2):
                block = pair[:, SUB * i : SUB * (i + 1), :].reshape(cpd, LANES)
                at = r * part + i * LANES
                gate_a[at : at + LANES, grp * cpd : (grp + 1) * cpd] = block.T.astype(BF16)
            ring2.begin(r, grp)

    k_bulk = (nch - 2) * cpd

    def weights(lo, hi):
        return ow[lo // (2 * cpd) : hi // (2 * cpd)].reshape(hi - lo, 2 * ec)

    def mix(r):
        rows = slice(r * part, (r + 1) * part)
        o_acc[...] = jnp.dot(gate_a[rows, 0:k_bulk], weights(0, k_bulk), preferred_element_type=F32)

    def finish(r):
        rows = slice(r * part, (r + 1) * part)
        total = o_acc[...] + jnp.dot(gate_a[rows, k_bulk:], weights(k_bulk, nch * cpd), preferred_element_type=F32)
        left, right = total[:, :ec].astype(BF16), total[:, ec:].astype(BF16)
        o_far[r] = jnp.where(xl == 0, right, left)
        mine = out.at[pl.ds(pl.multiple_of(xl * half + r * part, part), part), :]
        go(remote(o_far.at[r], mine, out_send.at[r], out_recv.at[r], s, partner))
        o_own[r] = jnp.where(xl == 0, left, right)
        pltpu.make_async_copy(o_own.at[r], mine, load_sem.at[18 + r]).start()

    repack(0)
    ow_last()
    order = []
    for t in range(1, hops + 2):
        if t <= hops:
            order.append((0, t))
        order.append((1, t - 1))
    for r, k in order:
        if k == 0:
            repack(r)
            continue
        if k == hops:
            mix(r)
        ring2.step(r, k)
        if k == hops:
            finish(r)

    for cp in sent:
        cp.wait_send()
    for i in range(2):
        arrived(w_all.at[0 : quarter * ds, wide : 2 * wide], w_send.at[i])
        arrived(proj_s.at[0 : peers - 1, i], a2a_send.at[1 + i])
        mine = out.at[pl.ds(pl.multiple_of(xl * half + i * part, part), part), :]
        theirs = out.at[pl.ds(pl.multiple_of(other * half + i * part, part), part), :]
        arrived(mine, load_sem.at[18 + i])
        arrived(theirs, out_recv.at[i])
    arrived(spec_s.at[0 : ns - 1], a2a_send.at[0])
    arrived(gate_s.at[0 : peers - 1], a2a_send.at[3])
    legs = ow.at[0 : nz - 1, 0, row, sides[0][1]] if plan.x_hi == 2 else ow.at[0 : nz - 1, 0, row, :]
    arrived(legs, ow_send.at[0])


def make(plan):
    consts = tables(plan)

    def shards(tokens, in_weight, conv_weight, spectrum, skip, out_weight):
        ns, peers, cpd = plan.ns, 2 * plan.ns, plan.cpd
        hops = plan.nz // 2
        vm = pltpu.VMEM
        dma = pltpu.SemaphoreType.DMA
        anywhere = pl.BlockSpec(memory_space=pl.ANY)
        scalars = pl.BlockSpec(memory_space=pltpu.SMEM)
        return pl.pallas_call(
            lambda *refs: kernel(plan, *refs),
            out_shape=jax.ShapeDtypeStruct((plan.tok, plan.ec), BF16),
            in_specs=[anywhere] * 10 + [scalars] * 2,
            out_specs=anywhere,
            scratch_shapes=[
                vm((plan.d, 6 * cpd), BF16),
                vm((plan.half, plan.d), BF16),
                vm((plan.half // 2, 6 * cpd), F32),
                vm((2, 2, cpd, plan.k2), F32), vm((plan.k2, plan.k2), BF16),
                vm((ns, 2, plan.m, 16, LANES), BF16), vm((ns, 2, plan.m, 16, LANES), BF16),
                vm((2, plan.m * ns * 16, LANES), F32),
                vm((peers, 2, 3, 16, LANES), BF16), vm((peers, 2, 3, 16, LANES), BF16),
                vm((3, plan.nhi * SUB, LANES), F32),
                vm((plan.nhi * SUB, LANES), F32),
                vm((peers, plan.rows, LANES), BF16), vm((peers, plan.rows, LANES), BF16),
                vm((plan.half, plan.nch * cpd), BF16),
                vm((plan.nz, 2, cpd, 2 * plan.ec), BF16),
                vm((plan.half // 2, 2 * plan.ec), F32),
                vm((2, plan.half // 2, plan.ec), BF16), vm((2, plan.half // 2, plan.ec), BF16),
                vm((2 * plan.ka, plan.nhi), BF16), vm((plan.nhi, 2 * plan.ka), BF16),
                vm((2, plan.ka, LANES), F32),
                vm((2 * LANES, 2 * LANES), BF16), vm((2 * LANES, 2 * LANES), BF16),
                dma((20,)), dma((2, 2, 2, hops)), dma((2, 2, 2, hops)), dma((2, 2, 2, hops)), dma((2, 2, 2, hops)),
                dma((2,)), dma((2,)), dma((3,)), dma((3,)), dma((4,)), dma((4,)),
                dma((plan.n_y + 4,)), dma((plan.n_y + 4,)), dma((2,)), dma((2,)),
            ],
            compiler_params=pltpu.CompilerParams(
                collective_id=0, has_side_effects=True, vmem_limit_bytes=56 * 1024 * 1024
            ),
            name="hyena",
        )(tokens, in_weight, spectrum, out_weight, *consts, conv_weight, skip)

    return shards


def on_mesh(mesh, plan):
    placed = (
        P("seq", "chan"),
        P(None, None, "chan"),
        P(None, None, "chan"),
        P(None, "chan", "seq", None),
        P("chan"),
        P("chan", None),
    )
    return jax.shard_map(make(plan), mesh=mesh, in_specs=placed, out_specs=P("seq", "chan"), check_vma=False)


def solution(mesh):
    return on_mesh(mesh, Plan(ns=16, nch=16, n_y=4, x_hi=2, tok=1024, ds=256, ec=256))
```

time: 125 us -> 116 us (0.928)
  Pallas kernels: 119 us -> 114 us
  other arithmetic: 2.31 us -> 0 us
    pallas_call x1, Pallas kernels: 119 us -> 114 us  [shards(): pl.pallas_call(lambda *refs: kernel(plan, *refs), out_shape=jax.ShapeDtyp...]
    convert_element_type x1 -> x0, other arithmetic: 2.31 us -> none  [shards(): spec = spectrum.reshape(2, 2 * plan.cpd, plan.k2).astype(BF16)]
where the time goes in v2:
time: 116 us
  Pallas kernels  114 us (98%)
  local copies, waits for them, and re-layouts  1.87 us (2%)
    pallas_call x1, Pallas kernels, shards(): pl.pallas_call(lambda *refs: kernel(plan, *refs), out_shape=jax.ShapeDtyp...  114 us

profile of v2, /device:TPU:2, one launch (start us, length us, event | category | flops | bytes accessed | tf_op | source)
XLA Modules:
  0.0 115.6 jit_solution(3322749458661900656)
XLA Ops:
  0.0 113.7 %hyena.1 = bf16[1024,256]{1,0:T(8,128)(2,1)} custom-call(bf16[1024,256]{1,0:T(8,128)(2,1)} %refs_0_.1, bf16[3,4096,128]{2,1,0:T(8,128)(2,1)} %refs_1_.1, f32[2,128,2,1024]{3,2,1,0:T(2,128)} %refs_2_.1, bf16[128,4096]{1,0:T(8,128)(2,1)} %refs_3_.1, bf16[512,128]{1,0:T(8,128)(2,1)} %constant.12.clone.refs_4_, bf16[128,512]{1,0:T(8,128)(2,1)} %constant.13.clone.refs_5_, ...), custom_call_target="tpu_custom_call" | custom-call | tf_op jit(solution)/shard_map/hyena/pallas_call | solution.py:499
  113.7 1.9 %copy.14 = bf16[1024,256]{1,0:T(8,128)(2,1)} copy(bf16[1024,256]{1,0:T(8,128)(2,1)} %hyena.1) | data formatting | bytes 1048576

commit v3 on v2

--- a/solution.py
+++ b/solution.py
@@ -114,6 +114,17 @@
         for p in range(2) for k in range(2)
     ]
 
+    def hop(by, size):
+        return min(by, size - by)
+
+    others = [(dy, dh, dl, dk) for dy in range(n_y) for dh in range(plan.x_hi) for dl in range(2) for dk in range(2)]
+    others = sorted(others[1:], key=lambda o: -hop(o[0], n_y) - (2 if o[1] and not o[2] else int(bool(o[1] or o[2]))))
+
+    def peer(o):
+        dy, dh, dl, dk = o
+        seq = seq_of(lax.rem(y + dy, n_y), lax.rem(xh + dh, plan.x_hi), lax.rem(core + dk, 2))
+        return seq, xl if dl == 0 else other
+
     bar = pltpu.get_barrier_semaphore()
 
     def greet_plane(d, carry):
@@ -142,12 +153,13 @@
         sent.append(cp)
 
     class Ring:
-        def __init__(self, buf, width, send, recv):
-            self.buf, self.width, self.send, self.recv = buf, width, send, recv
+        def __init__(self, buf, width, parts, send, recv):
+            self.buf, self.width, self.parts, self.send, self.recv = buf, width, parts, send, recv
 
         def item(self, r, way, grp, k):
             at = place(grp, (nz - k if way == 0 else k) % nz)
-            return self.buf.at[r * part : (r + 1) * part, at * self.width : (at + 1) * self.width]
+            lo, hi = self.parts[r]
+            return self.buf.at[lo:hi, at * self.width : (at + 1) * self.width]
 
         def hand_on(self, r, way, grp, k, src=None):
             to = lax.rem(z + 1, nz) if way == 0 else lax.rem(z + nz - 1, nz)
@@ -172,7 +184,7 @@
     def token_rows(side, r):
         return tokens.at[pl.ds(pl.multiple_of(side * half + r * part, part), part), :]
 
-    ring = Ring(tok_v, ds, ring_send, ring_recv)
+    ring = Ring(tok_v, ds, [(0, part), (part, half)], ring_send, ring_recv)
     far_home = tok_v.at[:, ds : 2 * ds]
 
     def swap(r):
@@ -181,6 +193,7 @@
     swap(0)
     ring.begin(0, 0, token_rows(xl, 0))
     swap(1)
+    ring.begin(1, 0, token_rows(xl, 1))
 
     quarter = nch // 4
 
@@ -243,21 +256,21 @@
         remote(spec_s.at[q], spec_r.at[s], a2a_send.at[0], a2a_recv.at[0], q, c).start()
         return carry
 
+    lax.fori_loop(1, ns, send_spec, 0)
+
     def pack(value, r, g, p):
         pair = [value[i * LANES : (i + 1) * LANES, :].T.reshape(ns, SUB, LANES) for i in range(2)]
         at = xl if g == 0 else other
         proj_s[pl.ds(at * ns, ns), r, p] = jnp.concatenate(pair, axis=1).astype(BF16)
 
     def send_proj(r, g):
-        def one(d, carry):
-            q = lax.rem(s + d, ns)
-            remote(
-                proj_s.at[(xl if g == 0 else other) * ns + q, r], proj_r.at[here, r], a2a_send.at[1 + r], a2a_recv.at[1 + r],
-                q, c if g == 0 else partner,
-            ).start()
-            return carry
-
-        lax.fori_loop(1 - g, ns, one, 0)
+        for o in others:
+            seq, side = peer(o)
+            if o[2] == g:
+                remote(
+                    proj_s.at[side * ns + seq, r], proj_r.at[here, r], a2a_send.at[1 + r], a2a_recv.at[1 + r],
+                    seq, side * nz + z,
+                ).start()
         if g == 0:
             pltpu.make_async_copy(proj_s.at[me, r], proj_r.at[here, r], load_sem.at[15 + r]).start()
 
@@ -316,42 +329,39 @@
         away = pl.ds(pl.multiple_of((1 - core) * 2 * quarter * ds, 2 * quarter * ds), 2 * quarter * ds)
         arrived(w_all.at[away, wide : 2 * wide], w_recv.at[2])
 
-    for k in range(1, hops + 1):
-        ring.step(0, k)
-        if k == max(hops - 1, 1):
-            arrived(far_home.at[part : 2 * part, :], x_recv.at[1])
-            ring.begin(1, 0, token_rows(xl, 1))
-            ring.begin(1, 1)
-        if k == 1:
-            ow_second()
-    loads[0].wait()
-    arrived(w_all.at[:, 0:wide], load_sem.at[1])
-    ow_third()
-    project(0, 0)
-    for k in range(1, hops):
-        ring.step(1, k)
-        if k == 1:
-            far_pass()
-            lax.fori_loop(1, ns, send_spec, 0)
-        if k == 2:
-            far_wait()
-            project(0, 1)
-    if hops < 2:
-        far_pass()
-        lax.fori_loop(1, ns, send_spec, 0)
-    if hops < 3:
-        far_wait()
-        project(0, 1)
-    ow_fourth()
+    def own_wait():
+        loads[0].wait()
+        arrived(w_all.at[:, 0:wide], load_sem.at[1])
+
+    def begin_second():
+        arrived(far_home.at[part : 2 * part, :], x_recv.at[1])
+        ring.begin(1, 1)
+
     bulk = (nch - 2) * ds
     rows = slice(part, 2 * part)
-    for g in range(2):
-        for p in range(3):
-            at = g * wide + p * cpd
-            if (at // cpd) % 2 == 0:
-                acc[:, at : at + 2 * cpd] = jnp.dot(
-                    tok_v[rows, 0:bulk], w_all[0:bulk, at : at + 2 * cpd], preferred_element_type=F32)
-    ring.step(1, hops)
+
+    def bulk_second():
+        for at in range(0, 2 * wide, 2 * cpd):
+            acc[:, at : at + 2 * cpd] = jnp.dot(
+                tok_v[rows, 0:bulk], w_all[0:bulk, at : at + 2 * cpd], preferred_element_type=F32)
+
+    after = {}
+    steps = sorted((k + r * (hops - 1), r, k) for r in range(2) for k in range(1, hops + 1))
+    place_of = {(r, k): i for i, (_, r, k) in enumerate(steps)}
+
+    def hook(r, k, *does):
+        k = max(1, min(k, hops))
+        after.setdefault(place_of[r, k], []).extend(does)
+
+    hook(0, hops - 1, begin_second, ow_second)
+    hook(0, hops, own_wait, lambda: project(0, 0))
+    hook(1, min(1, hops - 1), far_pass)
+    hook(1, min(2, hops - 1), far_wait, lambda: project(0, 1))
+    hook(1, hops - 1, bulk_second)
+    for i, (_, r, k) in enumerate(steps):
+        ring.step(r, k)
+        for do in after.get(i, []):
+            do()
     rest = acc[...] + jnp.dot(tok_v[rows, bulk:], w_all[bulk:, :], preferred_element_type=F32)
     for g in range(2):
         for p in range(3):
@@ -374,8 +384,9 @@
     for r in range(2):
         arrived(proj_r.at[here, r], load_sem.at[15 + r])
         arrived(proj_r.at[0 : peers - 1, r], a2a_recv.at[1 + r])
-    for p in range(3):
-        proj_f[p] = proj_r[:, :, p].astype(F32).reshape(plan.nhi * SUB, LANES)
+        for p in range(3):
+            for q in range(peers):
+                proj_f[p, q * plan.rows + 16 * r : q * plan.rows + 16 * (r + 1), :] = proj_r[q, r, p].astype(F32)
 
     lane = lax.broadcasted_iota(jnp.int32, (plan.nhi, LANES), 1)
     posn = lane + LANES * lax.broadcasted_iota(jnp.int32, (plan.nhi, LANES), 0)
@@ -413,26 +424,24 @@
     lax.fori_loop(0, SUB, transform, 0, unroll=True)
     gate_s[...] = gate_f[...].astype(BF16).reshape(peers, plan.rows, LANES)
 
-    def send_gate(d, carry):
-        q = lax.rem(here + d, peers)
-        remote(gate_s.at[q], gate_r.at[me], a2a_send.at[3], a2a_recv.at[3], q // 2, lax.rem(q, 2) * nz + z).start()
-        return carry
-
-    lax.fori_loop(1, peers, send_gate, 0)
+    for o in others:
+        seq, side = peer(o)
+        remote(gate_s.at[2 * seq + side], gate_r.at[me], a2a_send.at[3], a2a_recv.at[3], seq, side * nz + z).start()
     gate_own = pltpu.make_async_copy(gate_s.at[here], gate_r.at[me], load_sem.at[17])
     gate_own.start()
     gate_own.wait()
     arrived(gate_r.at[0 : peers - 1], a2a_recv.at[3])
 
-    ring2 = Ring(gate_a, cpd, ring2_send, ring2_recv)
+    parts2 = [(0, part), (part, half)]
+    ring2 = Ring(gate_a, cpd, parts2, ring2_send, ring2_recv)
 
     def repack(r):
+        lo, hi = parts2[r]
         for grp in range(2):
-            pair = gate_r[pl.ds((xl if grp == 0 else other) * ns, ns), 16 * r : 16 * (r + 1), :].astype(F32)
-            for i in range(2):
-                block = pair[:, SUB * i : SUB * (i + 1), :].reshape(cpd, LANES)
-                at = r * part + i * LANES
-                gate_a[at : at + LANES, grp * cpd : (grp + 1) * cpd] = block.T.astype(BF16)
+            for j in range(lo // LANES, hi // LANES):
+                rows = gate_r[pl.ds((xl if grp == 0 else other) * ns, ns), 16 * (j // 2) : 16 * (j // 2 + 1), :].astype(F32)
+                block = rows[:, SUB * (j % 2) : SUB * (j % 2 + 1), :].reshape(cpd, LANES)
+                gate_a[j * LANES : (j + 1) * LANES, grp * cpd : (grp + 1) * cpd] = block.T.astype(BF16)
             ring2.begin(r, grp)
 
     k_bulk = (nch - 2) * cpd
@@ -441,31 +450,34 @@
         return ow[lo // (2 * cpd) : hi // (2 * cpd)].reshape(hi - lo, 2 * ec)
 
     def mix(r):
-        rows = slice(r * part, (r + 1) * part)
-        o_acc[...] = jnp.dot(gate_a[rows, 0:k_bulk], weights(0, k_bulk), preferred_element_type=F32)
+        lo, hi = parts2[r]
+        o_acc[lo:hi, :] = jnp.dot(gate_a[lo:hi, 0:k_bulk], weights(0, k_bulk), preferred_element_type=F32)
+
+    def own_rows(side, r):
+        lo, hi = parts2[r]
+        return out.at[pl.ds(pl.multiple_of(side * half + lo, LANES), hi - lo), :]
 
     def finish(r):
-        rows = slice(r * part, (r + 1) * part)
-        total = o_acc[...] + jnp.dot(gate_a[rows, k_bulk:], weights(k_bulk, nch * cpd), preferred_element_type=F32)
+        lo, hi = parts2[r]
+        total = o_acc[lo:hi, :] + jnp.dot(gate_a[lo:hi, k_bulk:], weights(k_bulk, nch * cpd), preferred_element_type=F32)
         left, right = total[:, :ec].astype(BF16), total[:, ec:].astype(BF16)
-        o_far[r] = jnp.where(xl == 0, right, left)
-        mine = out.at[pl.ds(pl.multiple_of(xl * half + r * part, part), part), :]
-        go(remote(o_far.at[r], mine, out_send.at[r], out_recv.at[r], s, partner))
-        o_own[r] = jnp.where(xl == 0, left, right)
-        pltpu.make_async_copy(o_own.at[r], mine, load_sem.at[18 + r]).start()
-
+        o_far[lo:hi, :] = jnp.where(xl == 0, right, left)
+        go(remote(o_far.at[lo:hi, :], own_rows(xl, r), out_send.at[r], out_recv.at[r], s, partner))
+        o_own[lo:hi, :] = jnp.where(xl == 0, left, right)
+        pltpu.make_async_copy(o_own.at[lo:hi, :], own_rows(xl, r), load_sem.at[18 + r]).start()
+
+    ow_third()
     repack(0)
-    ow_last()
-    order = []
-    for t in range(1, hops + 2):
-        if t <= hops:
-            order.append((0, t))
-        order.append((1, t - 1))
-    for r, k in order:
+    order = sorted((k, r, k) for r in range(2) for k in range(hops + 1) if r + k > 0)
+    for _, r, k in order:
         if k == 0:
             repack(r)
             continue
+        if (r, k) == (1, max(hops - 1, 1)):
+            ow_fourth()
         if k == hops:
+            if r == 0:
+                ow_last()
             mix(r)
         ring2.step(r, k)
         if k == hops:
@@ -476,14 +488,13 @@
     for i in range(2):
         arrived(w_all.at[0 : quarter * ds, wide : 2 * wide], w_send.at[i])
         arrived(proj_s.at[0 : peers - 1, i], a2a_send.at[1 + i])
-        mine = out.at[pl.ds(pl.multiple_of(xl * half + i * part, part), part), :]
-        theirs = out.at[pl.ds(pl.multiple_of(other * half + i * part, part), part), :]
-        arrived(mine, load_sem.at[18 + i])
-        arrived(theirs, out_recv.at[i])
     arrived(spec_s.at[0 : ns - 1], a2a_send.at[0])
     arrived(gate_s.at[0 : peers - 1], a2a_send.at[3])
     legs = ow.at[0 : nz - 1, 0, row, sides[0][1]] if plan.x_hi == 2 else ow.at[0 : nz - 1, 0, row, :]
     arrived(legs, ow_send.at[0])
+    for r in range(2):
+        arrived(own_rows(xl, r), load_sem.at[18 + r])
+        arrived(own_rows(other, r), out_recv.at[r])
 
 
 def make(plan):
@@ -514,14 +525,14 @@
                 vm((peers, plan.rows, LANES), BF16), vm((peers, plan.rows, LANES), BF16),
                 vm((plan.half, plan.nch * cpd), BF16),
                 vm((plan.nz, 2, cpd, 2 * plan.ec), BF16),
-                vm((plan.half // 2, 2 * plan.ec), F32),
-                vm((2, plan.half // 2, plan.ec), BF16), vm((2, plan.half // 2, plan.ec), BF16),
+                vm((plan.half, 2 * plan.ec), F32),
+                vm((plan.half, plan.ec), BF16), vm((plan.half, plan.ec), BF16),
                 vm((2 * plan.ka, plan.nhi), BF16), vm((plan.nhi, 2 * plan.ka), BF16),
                 vm((2, plan.ka, LANES), F32),
                 vm((2 * LANES, 2 * LANES), BF16), vm((2 * LANES, 2 * LANES), BF16),
-                dma((20,)), dma((2, 2, 2, hops)), dma((2, 2, 2, hops)), dma((2, 2, 2, hops)), dma((2, 2, 2, hops)),
+                dma((21,)), dma((2, 2, 2, hops)), dma((2, 2, 2, hops)), dma((3, 2, 2, hops)), dma((3, 2, 2, hops)),
                 dma((2,)), dma((2,)), dma((3,)), dma((3,)), dma((4,)), dma((4,)),
-                dma((plan.n_y + 4,)), dma((plan.n_y + 4,)), dma((2,)), dma((2,)),
+                dma((plan.n_y + 4,)), dma((plan.n_y + 4,)), dma((3,)), dma((3,)),
             ],
             compiler_params=pltpu.CompilerParams(
                 collective_id=0, has_side_effects=True, vmem_limit_bytes=56 * 1024 * 1024

time: 116 us -> 108 us (0.931)
  Pallas kernels: 114 us -> 106 us
    pallas_call x1, Pallas kernels: 114 us -> 106 us  [shards(): pl.pallas_call(lambda *refs: kernel(plan, *refs), out_shape=jax.ShapeDtyp...]
where the time goes in v3:
time: 108 us; the launch traced here: 107 us
  Pallas kernels  106 us (98%)
  local copies, waits for them, and re-layouts  1.87 us (2%)
    pallas_call x1, Pallas kernels, shards(): pl.pallas_call(lambda *refs: kernel(plan, *refs), out_shape=jax.ShapeDtyp...  106 us

profile of v3, /device:TPU:2, one launch (start us, length us, event | category | flops | bytes accessed | tf_op | source)
XLA Modules:
  0.0 107.4 jit_solution(696042629729446483)
XLA Ops:
  0.0 105.5 %hyena.1 = bf16[1024,256]{1,0:T(8,128)(2,1)} custom-call(bf16[1024,256]{1,0:T(8,128)(2,1)} %refs_0_.1, bf16[3,4096,128]{2,1,0:T(8,128)(2,1)} %refs_1_.1, f32[2,128,2,1024]{3,2,1,0:T(2,128)} %refs_2_.1, bf16[128,4096]{1,0:T(8,128)(2,1)} %refs_3_.1, bf16[512,128]{1,0:T(8,128)(2,1)} %constant.12.clone.refs_4_, bf16[128,512]{1,0:T(8,128)(2,1)} %constant.13.clone.refs_5_, ...), custom_call_target="tpu_custom_call" | custom-call | tf_op jit(solution)/shard_map/hyena/pallas_call | solution.py:510
  105.6 1.9 %copy.14 = bf16[1024,256]{1,0:T(8,128)(2,1)} copy(bf16[1024,256]{1,0:T(8,128)(2,1)} %hyena.1) | data formatting | bytes 1048576

commit v4 on v3

--- a/solution.py
+++ b/solution.py
@@ -127,17 +127,12 @@
 
     bar = pltpu.get_barrier_semaphore()
 
-    def greet_plane(d, carry):
-        q = lax.rem(me + d, peers)
-        pl.semaphore_signal(bar, inc=1, device_id={"seq": lax.rem(q, ns), "chan": (q // ns) * nz + z}, device_id_type=MESH)
-        return carry
-
-    def greet_line(d, carry):
-        pl.semaphore_signal(bar, inc=1, device_id={"seq": s, "chan": xl * nz + lax.rem(z + d, nz)}, device_id_type=MESH)
-        return carry
-
-    lax.fori_loop(1, peers, greet_plane, 0)
-    lax.fori_loop(1, nz, greet_line, 0)
+    for dz in range(1, nz):
+        there = xl * nz + lax.rem(z + dz, nz)
+        pl.semaphore_signal(bar, inc=1, device_id={"seq": s, "chan": there}, device_id_type=MESH)
+    for o in reversed(others):
+        seq, side = peer(o)
+        pl.semaphore_signal(bar, inc=1, device_id={"seq": seq, "chan": side * nz + z}, device_id_type=MESH)
     for cp in loads[:2] + spec_loads:
         cp.start()
     start_weights()
@@ -346,18 +341,18 @@
                 tok_v[rows, 0:bulk], w_all[0:bulk, at : at + 2 * cpd], preferred_element_type=F32)
 
     after = {}
-    steps = sorted((k + r * (hops - 1), r, k) for r in range(2) for k in range(1, hops + 1))
+    steps = sorted((k + r * (hops - 1.5), r, k) for r in range(2) for k in range(1, hops + 1))
     place_of = {(r, k): i for i, (_, r, k) in enumerate(steps)}
 
     def hook(r, k, *does):
         k = max(1, min(k, hops))
         after.setdefault(place_of[r, k], []).extend(does)
 
-    hook(0, hops - 1, begin_second, ow_second)
+    hook(0, 2, begin_second)
+    hook(1, 1, ow_second)
     hook(0, hops, own_wait, lambda: project(0, 0))
-    hook(1, min(1, hops - 1), far_pass)
-    hook(1, min(2, hops - 1), far_wait, lambda: project(0, 1))
-    hook(1, hops - 1, bulk_second)
+    hook(1, 2, far_pass)
+    hook(1, hops - 1, far_wait, lambda: project(0, 1), bulk_second)
     for i, (_, r, k) in enumerate(steps):
         ring.step(r, k)
         for do in after.get(i, []):
@@ -432,7 +427,8 @@
     gate_own.wait()
     arrived(gate_r.at[0 : peers - 1], a2a_recv.at[3])
 
-    parts2 = [(0, part), (part, half)]
+    n_parts = 4
+    parts2 = [(i * half // n_parts, (i + 1) * half // n_parts) for i in range(n_parts)]
     ring2 = Ring(gate_a, cpd, parts2, ring2_send, ring2_recv)
 
     def repack(r):
@@ -449,9 +445,8 @@
     def weights(lo, hi):
         return ow[lo // (2 * cpd) : hi // (2 * cpd)].reshape(hi - lo, 2 * ec)
 
-    def mix(r):
-        lo, hi = parts2[r]
-        o_acc[lo:hi, :] = jnp.dot(gate_a[lo:hi, 0:k_bulk], weights(0, k_bulk), preferred_element_type=F32)
+    def mix():
+        o_acc[...] = jnp.dot(gate_a[:, 0:k_bulk], weights(0, k_bulk), preferred_element_type=F32)
 
     def own_rows(side, r):
         lo, hi = parts2[r]
@@ -468,20 +463,18 @@
 
     ow_third()
     repack(0)
-    order = sorted((k, r, k) for r in range(2) for k in range(hops + 1) if r + k > 0)
-    for _, r, k in order:
-        if k == 0:
-            repack(r)
-            continue
-        if (r, k) == (1, max(hops - 1, 1)):
-            ow_fourth()
-        if k == hops:
-            if r == 0:
-                ow_last()
-            mix(r)
-        ring2.step(r, k)
-        if k == hops:
-            finish(r)
+    for r in range(1, n_parts):
+        repack(r)
+    for k in range(1, hops):
+        for r in range(n_parts):
+            ring2.step(r, k)
+            if (k, r) == (max(hops - 2, 1), 3):
+                ow_fourth()
+    ow_last()
+    mix()
+    for r in range(n_parts):
+        ring2.step(r, hops)
+        finish(r)
 
     for cp in sent:
         cp.wait_send()
@@ -492,7 +485,7 @@
     arrived(gate_s.at[0 : peers - 1], a2a_send.at[3])
     legs = ow.at[0 : nz - 1, 0, row, sides[0][1]] if plan.x_hi == 2 else ow.at[0 : nz - 1, 0, row, :]
     arrived(legs, ow_send.at[0])
-    for r in range(2):
+    for r in range(n_parts):
         arrived(own_rows(xl, r), load_sem.at[18 + r])
         arrived(own_rows(other, r), out_recv.at[r])
 
@@ -530,9 +523,9 @@
                 vm((2 * plan.ka, plan.nhi), BF16), vm((plan.nhi, 2 * plan.ka), BF16),
                 vm((2, plan.ka, LANES), F32),
                 vm((2 * LANES, 2 * LANES), BF16), vm((2 * LANES, 2 * LANES), BF16),
-                dma((21,)), dma((2, 2, 2, hops)), dma((2, 2, 2, hops)), dma((3, 2, 2, hops)), dma((3, 2, 2, hops)),
+                dma((22,)), dma((2, 2, 2, hops)), dma((2, 2, 2, hops)), dma((4, 2, 2, hops)), dma((4, 2, 2, hops)),
                 dma((2,)), dma((2,)), dma((3,)), dma((3,)), dma((4,)), dma((4,)),
-                dma((plan.n_y + 4,)), dma((plan.n_y + 4,)), dma((3,)), dma((3,)),
+                dma((plan.n_y + 4,)), dma((plan.n_y + 4,)), dma((4,)), dma((4,)),
             ],
             compiler_params=pltpu.CompilerParams(
                 collective_id=0, has_side_effects=True, vmem_limit_bytes=56 * 1024 * 1024

time: 108 us -> 104 us (0.963)
  Pallas kernels: 106 us -> 102 us
    pallas_call x1, Pallas kernels: 106 us -> 102 us  [shards(): pl.pallas_call(lambda *refs: kernel(plan, *refs), out_shape=jax.ShapeDtyp...]
where the time goes in v4:
time: 104 us
  Pallas kernels  102 us (98%)
  local copies, waits for them, and re-layouts  1.87 us (2%)
    pallas_call x1, Pallas kernels, shards(): pl.pallas_call(lambda *refs: kernel(plan, *refs), out_shape=jax.ShapeDtyp...  102 us

profile of v4, /device:TPU:2, one launch (start us, length us, event | category | flops | bytes accessed | tf_op | source)
XLA Modules:
  0.0 104.3 jit_solution(5821134241106567984)
XLA Ops:
  0.0 102.4 %hyena.1 = bf16[1024,256]{1,0:T(8,128)(2,1)} custom-call(bf16[1024,256]{1,0:T(8,128)(2,1)} %refs_0_.1, bf16[3,4096,128]{2,1,0:T(8,128)(2,1)} %refs_1_.1, f32[2,128,2,1024]{3,2,1,0:T(2,128)} %refs_2_.1, bf16[128,4096]{1,0:T(8,128)(2,1)} %refs_3_.1, bf16[512,128]{1,0:T(8,128)(2,1)} %constant.12.clone.refs_4_, bf16[128,512]{1,0:T(8,128)(2,1)} %constant.13.clone.refs_5_, ...), custom_call_target="tpu_custom_call" | custom-call | tf_op jit(solution)/shard_map/hyena/pallas_call | solution.py:503
  102.4 1.9 %copy.14 = bf16[1024,256]{1,0:T(8,128)(2,1)} copy(bf16[1024,256]{1,0:T(8,128)(2,1)} %hyena.1) | data formatting | bytes 1048576

commit v5 on v4

--- a/solution.py
+++ b/solution.py
@@ -391,17 +391,17 @@
         both = jnp.where(lane < by, pltpu.roll(turned, 1, 0), turned)
         return jnp.where(posn < by, 0.0, both)
 
-    def transform(ch, carry):
-        chan = s * SUB + ch
+    def streams(ch):
         parts = []
         for p in range(3):
             x = proj_f[p, pl.ds(ch, plan.nhi, stride=SUB), :]
-            f = conv_w[0, p, chan] * x
+            f = conv_w[0, p, s * SUB + ch] * x
             for j in range(1, 3):
-                f = f + conv_w[j, p, chan] * behind(x, j)
+                f = f + conv_w[j, p, s * SUB + ch] * behind(x, j)
             parts.append(f)
-        query, signal = parts[0], (parts[1] * parts[2]).astype(BF16)
-        a = jnp.dot(f1[...], signal, preferred_element_type=F32)
+        return parts[0], (parts[1] * parts[2]).astype(BF16)
+
+    def middle(ch, a):
         ar, ai = a[: plan.ka], a[plan.ka :]
         tr, ti = tw[0], tw[1]
         yy = jnp.concatenate([(ar * tr - ai * ti).astype(BF16), (ar * ti + ai * tr).astype(BF16)], axis=1)
@@ -411,12 +411,17 @@
         pp = jnp.concatenate([(zr * hr - zi * hi).astype(BF16), (zr * hi + zi * hr).astype(BF16)], axis=1)
         u = jnp.dot(pp, g2[...], preferred_element_type=F32)
         ur, ui = u[:, :LANES], u[:, LANES:]
-        v = jnp.concatenate([(ur * tr + ui * ti).astype(BF16), (ui * tr - ur * ti).astype(BF16)], axis=0)
+        return jnp.concatenate([(ur * tr + ui * ti).astype(BF16), (ui * tr - ur * ti).astype(BF16)], axis=0)
+
+    for ch in range(0, SUB, 2):
+        both = [streams(ch + i) for i in range(2)]
+        a = jnp.dot(f1[...], jnp.concatenate([signal for _, signal in both], axis=1), preferred_element_type=F32)
+        v = jnp.concatenate([middle(ch + i, a[:, i * LANES : (i + 1) * LANES]) for i in range(2)], axis=1)
         longconv = jnp.dot(g1[...], v, preferred_element_type=F32)
-        gate_f[pl.ds(ch, plan.nhi, stride=SUB), :] = query * (longconv + skip_w[chan] * signal.astype(F32))
-        return carry
-
-    lax.fori_loop(0, SUB, transform, 0, unroll=True)
+        for i, (query, signal) in enumerate(both):
+            direct = skip_w[s * SUB + ch + i] * signal.astype(F32)
+            gate_f[pl.ds(ch + i, plan.nhi, stride=SUB), :] = query * (longconv[:, i * LANES : (i + 1) * LANES] + direct)
+
     gate_s[...] = gate_f[...].astype(BF16).reshape(peers, plan.rows, LANES)
 
     for o in others:

time: 104 us -> 104 us (level)
  no operation moved by 1% of the time
where the time goes in v5:
time: 104 us; the launch traced here: 103 us
  Pallas kernels  102 us (98%)
  local copies, waits for them, and re-layouts  1.87 us (2%)
    pallas_call x1, Pallas kernels, shards(): pl.pallas_call(lambda *refs: kernel(plan, *refs), out_shape=jax.ShapeDtyp...  102 us

profile of v5, /device:TPU:2, one launch (start us, length us, event | category | flops | bytes accessed | tf_op | source)
XLA Modules:
  0.0 103.4 jit_solution(9027659551082630331)
XLA Ops:
  0.0 101.6 %hyena.1 = bf16[1024,256]{1,0:T(8,128)(2,1)} custom-call(bf16[1024,256]{1,0:T(8,128)(2,1)} %refs_0_.1, bf16[3,4096,128]{2,1,0:T(8,128)(2,1)} %refs_1_.1, f32[2,128,2,1024]{3,2,1,0:T(2,128)} %refs_2_.1, bf16[128,4096]{1,0:T(8,128)(2,1)} %refs_3_.1, bf16[512,128]{1,0:T(8,128)(2,1)} %constant.12.clone.refs_4_, bf16[128,512]{1,0:T(8,128)(2,1)} %constant.13.clone.refs_5_, ...), custom_call_target="tpu_custom_call" | custom-call | tf_op jit(solution)/shard_map/hyena/pallas_call | solution.py:508
  101.6 1.9 %copy.14 = bf16[1024,256]{1,0:T(8,128)(2,1)} copy(bf16[1024,256]{1,0:T(8,128)(2,1)} %hyena.1) | data formatting | bytes 1048576

commit v6 on v5

--- a/solution.py
+++ b/solution.py
@@ -357,11 +357,11 @@
         ring.step(r, k)
         for do in after.get(i, []):
             do()
-    rest = acc[...] + jnp.dot(tok_v[rows, bulk:], w_all[bulk:, :], preferred_element_type=F32)
     for g in range(2):
+        half_of = slice(g * wide, (g + 1) * wide)
+        rest = acc[:, half_of] + jnp.dot(tok_v[rows, bulk:], w_all[bulk:, half_of], preferred_element_type=F32)
         for p in range(3):
-            at = g * wide + p * cpd
-            pack(rest[:, at : at + cpd], 1, g, p)
+            pack(rest[:, p * cpd : (p + 1) * cpd], 1, g, p)
         send_proj(1, g)
 
     spec_own.wait()

time: 104 us -> 104 us (level)
  no operation moved by 1% of the time
where the time goes in v6:
time: 104 us
  Pallas kernels  102 us (98%)
  local copies, waits for them, and re-layouts  1.87 us (2%)
    pallas_call x1, Pallas kernels, shards(): pl.pallas_call(lambda *refs: kernel(plan, *refs), out_shape=jax.ShapeDtyp...  102 us

profile of v6, /device:TPU:2, one launch (start us, length us, event | category | flops | bytes accessed | tf_op | source)
XLA Modules:
  0.0 103.5 jit_solution(9375434064885632483)
XLA Ops:
  0.0 101.6 %hyena.1 = bf16[1024,256]{1,0:T(8,128)(2,1)} custom-call(bf16[1024,256]{1,0:T(8,128)(2,1)} %refs_0_.1, bf16[3,4096,128]{2,1,0:T(8,128)(2,1)} %refs_1_.1, f32[2,128,2,1024]{3,2,1,0:T(2,128)} %refs_2_.1, bf16[128,4096]{1,0:T(8,128)(2,1)} %refs_3_.1, bf16[512,128]{1,0:T(8,128)(2,1)} %constant.12.clone.refs_4_, bf16[128,512]{1,0:T(8,128)(2,1)} %constant.13.clone.refs_5_, ...), custom_call_target="tpu_custom_call" | custom-call | tf_op jit(solution)/shard_map/hyena/pallas_call | solution.py:508
  101.6 1.9 %copy.14 = bf16[1024,256]{1,0:T(8,128)(2,1)} copy(bf16[1024,256]{1,0:T(8,128)(2,1)} %hyena.1) | data formatting | bytes 1048576
